TPU v7x, 512 devices: a whole 4x4x16 slice. The times are simulated.
512 devices in a mesh: row: 16 (over y, x), col: 32 (over z, core).
Axes of the slice: x: 4, y: 4, z: 16, core: 2. Of those that a mesh axis runs over, the one named last changes fastest.
Arguments:
- inputs: bfloat16 [1024, 6144], P('col', 'row'), may hold values from -6 to 6
- cotangent: bfloat16 [1024, 6144], P('col', 'row'), may hold values from -0.59765625 to 0.59765625
- weight_in: bfloat16 [6144, 24576], P('row', 'col'), may hold values from -0.078125 to 0.078125
- weight_out: bfloat16 [24576, 6144], P('col', 'row'), may hold values from -0.078125 to 0.078125
Outputs:
- grad_inputs: bfloat16 [1024, 6144], P('col', 'row')
- grad_weight_in: float32 [6144, 24576], P('row', 'col')
- grad_weight_out: float32 [24576, 6144], P('col', 'row')
All inputs are finite; a program needn't handle non-finite values.
Results may differ from a plain program's by a relative error of at most 0.0049.
Values may be sent and summed in bfloat16 or wider, within the bound.
No kernel may reach another device: no remote copies, remote signals or barrier semaphores. Data moves between devices by JAX's collectives and lax.ppermute only.
A program may use at most 64 MiB of HBM per device.

v0:
```python
import jax
import jax.numpy as jnp
from jax import lax
from jax.sharding import PartitionSpec as P

inv_sqrt_two = 0.7071067811865476
inv_sqrt_two_pi = 0.3989422804014327


def gelu_backward(preact, act_grad):
    normal_cdf = 0.5 * (1.0 + lax.erf(preact * inv_sqrt_two))
    normal_pdf = jnp.exp(-0.5 * preact * preact) * inv_sqrt_two_pi
    activated = (preact * normal_cdf).astype(jnp.bfloat16)
    pre_grad = (act_grad * (normal_cdf + preact * normal_pdf)).astype(jnp.bfloat16)
    return (activated, pre_grad)


def body(inputs, cotangent, weight_in, weight_out):
    gathered_in, gathered_cot = (
        lax.all_gather(inputs, "col", axis=0, tiled=True),
        lax.all_gather(cotangent, "col", axis=0, tiled=True),
    )
    pre_part = jnp.dot(gathered_in, weight_in, preferred_element_type=jnp.float32)
    grad_part = lax.dot_general(
        gathered_cot, weight_out, (((1,), (1,)), ((), ())), preferred_element_type=jnp.float32
    )
    preact, act_grad = lax.psum((pre_part, grad_part), "row")
    activated, pre_grad = gelu_backward(preact, act_grad)
    grad_weight_out = lax.dot_general(
        activated, gathered_cot, (((0,), (0,)), ((), ())), preferred_element_type=jnp.float32
    )
    grad_weight_in = lax.dot_general(
        gathered_in, pre_grad, (((0,), (0,)), ((), ())), preferred_element_type=jnp.float32
    )
    summed = lax.psum_scatter(
        lax.dot_general(
            pre_grad, weight_in, (((1,), (1,)), ((), ())), preferred_element_type=jnp.float32
        ),
        "col",
        scatter_dimension=0,
        tiled=True,
    )
    grad_inputs = summed.astype(jnp.bfloat16)
    return (grad_inputs, grad_weight_in, grad_weight_out)


def solution(mesh):
    placed = (P("col", "row"), P("col", "row"), P("row", "col"), P("col", "row"))
    return jax.shard_map(
        body,
        mesh=mesh,
        in_specs=placed,
        out_specs=(P("col", "row"), P("row", "col"), P("col", "row")),
        check_vma=False,
    )
```

profile of v0, /device:TPU:1, one launch (start us, length us, event | category | flops | bytes accessed | tf_op | source)
XLA Modules:
  0.0 352.9 jit_solution(3817607588521012312)
XLA Ops:
  7.2 0.0 copy-start
  7.2 0.0 all-reduce.3.cloned.1.call-start
  7.2 40.1 %all_gather.7 = bf16[1024,384]{1,0:T(8,128)(2,1)S(1)} all-gather(bf16[32,384]{1,0:T(8,128)(2,1)} %param.4), channel_id=1, replica_groups=mesh['row'=16,'col'=32] {'col'}, dimensions={0}, use_global_device_ids=true | all-gather | bytes 811008 | tf_op jit(solution)/shard_map/all_gather | solution.py:20
  47.3 0.0 copy-start.1
  47.3 29.5 %all_gather.6 = bf16[1024,384]{1,0:T(8,128)(2,1)S(1)} all-gather(bf16[32,384]{1,0:T(8,128)(2,1)} %param.5), channel_id=1, replica_groups=mesh['row'=16,'col'=32] {'col'}, dimensions={0}, use_global_device_ids=true | all-gather | bytes 811008 | tf_op jit(solution)/shard_map/all_gather | solution.py:21
  76.8 3.8 %fusion.7 = f32[1024,768]{1,0:T(8,128)} fusion(bf16[1024,384]{1,0:T(8,128)(2,1)S(1)} %all_gather.6, bf16[768,384]{1,0:T(8,128)(2,1)} %param.7), kind=kOutput, calls=%fused_computation.11 | convolution fusion | flops 603979776 | bytes 4521984 | tf_op jit(solution)/shard_map/dot_general | solution.py:24
  80.5 0.0 copy-done.1
  80.6 0.0 copy-done
  80.6 2.6 fusion.8
  83.2 0.0 all-reduce.3.cloned.1.call-update
  83.2 0.0 reduce-scatter.2.cloned.1.call-start
  83.2 149.5 %all-reduce.3.cloned.1.call-done = (f32[1024,768]{1,0:T(8,128)}, f32[1024,768]{1,0:T(8,128)}) async-done(((f32[1024,768]{1,0:T(8,128)}, f32[1024,768]{1,0:T(8,128)}), (f32[1024,768]{1,0:T(8,128)}, f32[1024,768]{1,0:T(8,128)})) %all-reduce.3.cloned.1.call-update) | async-done | bytes 6291472 | tf_op jit(solution)/shard_map/psum | solution.py:27
  232.7 3.5 fusion.5
  236.2 2.1 fusion.9
  238.4 0.0 reduce-scatter.2.cloned.1.call-update
  238.4 3.1 convolution_bitcast_fusion
  241.6 2.7 copy.7
  244.2 3.9 %fusion.6 = f32[768,384]{1,0:T(8,128)} fusion(bf16[1024,384]{1,0:T(8,128)(2,1)S(1)} %all_gather.6, f32[1024,768]{1,0:T(8,128)} %get-tuple-element.7), kind=kOutput, calls=%fused_computation.9 | convolution fusion | flops 607911936 | bytes 5111808 | tf_op jit(solution)/shard_map/dot_general | solution.py:29
  248.1 96.6 %reduce-scatter.2.cloned.1.call-done = f32[32,384]{1,0:T(8,128)} async-done(((f32[1024,384]{1,0:T(8,128)}), f32[32,384]{1,0:T(8,128)}) %reduce-scatter.2.cloned.1.call-update) | async-done | bytes 49168 | tf_op jit(solution)/shard_map/reduce_scatter | solution.py:35
  344.7 1.4 convert_element_type.10
Async XLA Ops:
  7.2 73.4 %copy-start = (bf16[384,768]{1,0:T(8,128)(2,1)S(1)}, bf16[384,768]{1,0:T(8,128)(2,1)}, u32[]{:S(2)}) copy-start(bf16[384,768]{1,0:T(8,128)(2,1)} %param.6) | copy-start | bytes 1769476
  7.2 225.6 %all-reduce.3.cloned.1.call-start = ((), (), s32[]{:S(2)}) async-start(), calls=%async_computation.2 | async-start | bytes 12582912 | tf_op jit(solution)/shard_map/psum | solution.py:27
  47.3 33.2 %copy-start.1 = (bf16[1024,384]{1,0:T(8,128)(2,1)}, bf16[1024,384]{1,0:T(8,128)(2,1)S(1)}, u32[]{:S(2)}) copy-start(bf16[1024,384]{1,0:T(8,128)(2,1)S(1)} %all_gather.7) | copy-start | bytes 2359300
  83.2 261.5 %reduce-scatter.2.cloned.1.call-start = ((), (), s32[]{:S(2)}) async-start(), calls=%async_computation.1 | async-start | bytes 1622016 | tf_op jit(solution)/shard_map/reduce_scatter | solution.py:35
Sparse Core Ops, SparseCore 0:
  83.3 149.3 all-reduce.2
  238.5 106.1 reduce-scatter.1
where the time goes:
time: 355 us; the launch traced here: 353 us
  waiting for transfers between devices  246 us (69%)
  blocking collectives  69.6 us (20%)
  matrix products  15.6 us (4%)
  between operations  14.1 us (4%)
  other arithmetic  4.9 us (1%)
    psum x1, waiting for transfers between devices, body(): preact, act_grad = lax.psum((pre_part, grad_part), 'row')  150 us
    reduce_scatter x1, waiting for transfers between devices, body(): lax.psum_scatter(lax.dot_general(pre_grad, weight_in, (((1,), (1,)), ((),...  96.6 us
    all_gather x1, blocking collectives, body(): lax.all_gather(inputs, 'col', axis=0, tiled=True)  40.1 us
    all_gather x1, blocking collectives, body(): lax.all_gather(cotangent, 'col', axis=0, tiled=True)  29.5 us
  transfers between devices with their start and end apart: 2, of which 2 were waited for; matrix products, arithmetic and copies ran while one was open for 3% of the time, Pallas kernels for 0%

commit v1 on v0

v1 whole, which is shorter than its diff:
```python
import jax
import jax.numpy as jnp
import numpy as np
from jax import lax
from jax.sharding import Mesh
from jax.sharding import PartitionSpec as P

inv_sqrt_two = 0.7071067811865476
inv_sqrt_two_pi = 0.3989422804014327
ROW = ("y", "x")
COL = ("z", "core")
SWAP = [(0, 1), (1, 0)]


def gelu_backward(preact, act_grad):
    normal_cdf = 0.5 * (1.0 + lax.erf(preact * inv_sqrt_two))
    normal_pdf = jnp.exp(-0.5 * preact * preact) * inv_sqrt_two_pi
    activated = (preact * normal_cdf).astype(jnp.bfloat16)
    pre_grad = (act_grad * (normal_cdf + preact * normal_pdf)).astype(jnp.bfloat16)
    return (activated, pre_grad)


def dot(a, b, ca, cb):
    return lax.dot_general(a, b, (((ca,), (cb,)), ((), ())), preferred_element_type=jnp.float32)


def body(inputs, cotangent, weight_in, weight_out):
    rows, depth = inputs.shape
    hidden = weight_in.shape[1]
    n_row = lax.axis_size(ROW)
    n_z = lax.axis_size("z")
    both = jnp.stack([inputs, cotangent])
    own = lax.all_gather(both, "z", axis=1, tiled=True)
    other = lax.ppermute(own, "core", SWAP)
    full = jnp.concatenate([own, other], axis=1)
    x, g = full[0], full[1]
    tokens = x.shape[0]
    share = tokens // n_row
    pre_part = dot(x, weight_in, 1, 0).astype(jnp.bfloat16)
    grad_part = dot(g, weight_out, 1, 1).astype(jnp.bfloat16)
    parts = jnp.stack(
        [pre_part.reshape(n_row, share, hidden), grad_part.reshape(n_row, share, hidden)], axis=1
    )
    landed = lax.all_to_all(parts, ROW, 0, 0, tiled=True)
    sums = jnp.sum(landed.astype(jnp.float32), axis=0)
    activated, pre_grad = gelu_backward(sums[0], sums[1])
    hid = lax.all_gather(jnp.stack([activated, pre_grad]), ROW, axis=1, tiled=True)
    act, pg = hid[0], hid[1]
    gi = dot(pg, weight_in, 1, 1)
    half = tokens // 2
    mine = gi[:half] + lax.ppermute(gi[half:], "core", SWAP)
    pieces = lax.all_to_all(
        mine.astype(jnp.bfloat16).reshape(n_z, rows, depth), "z", 0, 0, tiled=True
    )
    grad_inputs = jnp.sum(pieces.astype(jnp.float32), axis=0).astype(jnp.bfloat16)
    grad_weight_out = dot(act, g, 0, 0)
    grad_weight_in = dot(x, pg, 0, 0)
    return (grad_inputs, grad_weight_in, grad_weight_out)


def solution(mesh):
    split = Mesh(mesh.devices.reshape(4, 4, 16, 2), ROW + COL)
    tok, w_in, w_out = P(COL, ROW), P(ROW, COL), P(COL, ROW)
    return jax.shard_map(
        body,
        mesh=split,
        in_specs=(tok, tok, w_in, w_out),
        out_specs=(tok, w_in, w_out),
        check_vma=False,
    )
```

time: 355 us -> 210 us (0.59)
  the two profiles are of different devices: /device:TPU:1 before, /device:TPU:2 now
where the time goes in v1:
time: 210 us; the launch traced here: 209 us
  blocking collectives  86 us (41%)
  waiting for transfers between devices  78.9 us (38%)
  starting transfers between devices  16.3 us (8%)
  between operations  14.1 us (7%)
  matrix products  9.78 us (5%)
  other arithmetic  3.82 us (2%)
    all_gather x1, waiting for transfers between devices, body(): lax.all_gather(jnp.stack([activated, pre_grad]), ROW, axis=1, tiled=True)  55.6 us
    all_to_all x1, blocking collectives, body(): landed = lax.all_to_all(parts, ROW, 0, 0, tiled=True)  45.8 us
    all_gather x1, blocking collectives, body(): own = lax.all_gather(both, 'z', axis=1, tiled=True)  40.1 us
    all_to_all x1, waiting for transfers between devices, body(): lax.all_to_all(mine.astype(jnp.bfloat16).reshape(n_z, rows, depth), 'z',...  18.9 us
    all_to_all x1, starting transfers between devices, body(): lax.all_to_all(mine.astype(jnp.bfloat16).reshape(n_z, rows, depth), 'z',...  12.3 us
    dot_general x5, matrix products, dot(): lax.dot_general(a, b, (((ca,), (cb,)), ((), ())), preferred_element_type=...  9.78 us
  transfers between devices with their start and end apart: 4, of which 4 were waited for; matrix products, arithmetic and copies ran while one was open for 3% of the time, Pallas kernels for 0%

profile of v1, /device:TPU:2, one launch (start us, length us, event | category | flops | bytes accessed | tf_op | source)
XLA Modules:
  0.0 209.2 jit_solution(8601400072918444326)
XLA Ops:
  7.2 0.8 pad_maximum_fusion.2
  8.0 40.1 %all_gather.6 = bf16[2,512,384]{2,1,0:T(8,128)(2,1)S(1)} all-gather(bf16[2,32,384]{2,1,0:T(8,128)(2,1)S(1)} %pad_maximum_fusion.2), channel_id=1, replica_groups=mesh['y'=4,'x'=4,'z'=16,'core'=2] {'z'}, dimensions={1}, use_global_device_ids=true | all-gather | bytes 835584 | tf_op jit(solution)/shard_map/all_gather | solution.py:33
  48.2 2.0 collective-permute-start
  50.2 0.1 constant_dynamic-update-slice_fusion.1
  50.3 2.2 %collective-permute-done = bf16[2,512,384]{2,1,0:T(8,128)(2,1)S(1)} collective-permute-done((bf16[2,512,384]{2,1,0:T(8,128)(2,1)S(1)}, bf16[2,512,384]{2,1,0:T(8,128)(2,1)S(1)}, u32[]{:S(2)}, u32[]{:S(2)}) %collective-permute-start) | collective-permute-done | bytes 786464 | tf_op jit(solution)/shard_map/ppermute | solution.py:34
  52.5 0.1 constant_dynamic-update-slice_fusion
  52.6 1.0 convolution_convert_fusion
  53.6 1.0 convolution_convert_fusion.1
  54.6 0.3 pad_maximum_fusion
  54.9 45.8 %all_to_all.10 = bf16[16,2,64,768]{3,2,1,0:T(8,128)(2,1)S(1)} all-to-all(bf16[16,2,64,768]{3,2,1,0:T(8,128)(2,1)S(1)} %pad_maximum_fusion), channel_id=1, replica_groups=mesh['y'=4,'x'=4,'z'=16,'core'=2] {'y','x'}, dimensions={0} | all-to-all | bytes 6291456 | tf_op jit(solution)/shard_map/all_to_all | solution.py:44
  100.8 0.4 convert_reduce_fusion
  101.2 0.1 multiply_convert_fusion
  101.3 0.7 pad_maximum_fusion.1
  102.0 55.6 %all-gather.2.cloned.1.call-done = bf16[2,1024,768]{2,1,0:T(8,128)(2,1)} async-done(((bf16[2,64,768]{2,1,0:T(8,128)(2,1)}), bf16[2,1024,768]{2,1,0:T(8,128)(2,1)}) %all-gather.2.cloned.1.call-update) | async-done | bytes 3145744 | tf_op jit(solution)/shard_map/all_gather | solution.py:47
  157.6 2.4 %fusion.2 = f32[1024,384]{1,0:T(8,128)S(1)} fusion(bf16[384,768]{1,0:T(8,128)(2,1)S(1)} %copy-done, bf16[2,1024,768]{2,1,0:T(8,128)(2,1)} %all-gather.2.cloned.1.call-done), kind=kOutput, calls=%fused_computation.8 | convolution fusion | flops 603979776 | bytes 3735552 | tf_op jit(solution)/shard_map/dot_general | solution.py:24
  160.0 0.1 slice.38
  160.1 1.9 collective-permute-start.1
  162.0 2.3 %collective-permute-done.1 = f32[512,384]{1,0:T(8,128)S(1)} collective-permute-done((f32[512,384]{1,0:T(8,128)S(1)}, f32[512,384]{1,0:T(8,128)S(1)}, u32[]{:S(2)}, u32[]{:S(2)}) %collective-permute-start.1) | collective-permute-done | bytes 786464 | tf_op jit(solution)/shard_map/ppermute | solution.py:51
  164.3 0.8 fusion.3
  165.1 12.3 %all-to-all-start.1 = ((bf16[16,32,384]{2,1,0:T(8,128)(2,1)}), bf16[16,32,384]{2,1,0:T(8,128)(2,1)S(1)}, u32[]{:S(2)}, u32[]{:S(2)}) async-start(bf16[16,32,384]{2,1,0:T(8,128)(2,1)} %bitcast.9), calls=%async_computation.1 | async-start | bytes 786432 | tf_op jit(solution)/shard_map/all_to_all | solution.py:52
  177.4 3.4 %fusion.1 = f32[384,768]{1,0:T(8,128)} fusion(bf16[2,1024,768]{2,1,0:T(8,128)(2,1)} %all-gather.2.cloned.1.call-done, bf16[2,1024,384]{2,1,0:T(8,128)(2,1)S(1)} %constant_dynamic-update-slice_fusion), kind=kOutput, calls=%fused_computation.7 | convolution fusion | flops 603979776 | bytes 3538944 | tf_op jit(solution)/shard_map/dot_general | solution.py:24
  180.8 2.0 fusion
  182.8 18.9 %all-to-all-done.1 = bf16[16,32,384]{2,1,0:T(8,128)(2,1)S(1)} async-done(((bf16[16,32,384]{2,1,0:T(8,128)(2,1)}), bf16[16,32,384]{2,1,0:T(8,128)(2,1)S(1)}, u32[]{:S(2)}, u32[]{:S(2)}) %all-to-all-start.1) | async-done | bytes 393248 | tf_op jit(solution)/shard_map/all_to_all | solution.py:52
  201.7 0.7 reduce_sum.22
  (8 shorter events, 0.1 us)
Async XLA Ops:
  7.2 46.5 %copy-start = (bf16[384,768]{1,0:T(8,128)(2,1)S(1)}, bf16[384,768]{1,0:T(8,128)(2,1)}, u32[]{:S(2)}) copy-start(bf16[384,768]{1,0:T(8,128)(2,1)} %param.6) | copy-start | bytes 1769476
  7.2 150.5 %all-gather.2.cloned.1.call-start = ((), (), s32[]{:S(2)}) async-start(), calls=%async_computation.2 | async-start | bytes 3342336 | tf_op jit(solution)/shard_map/all_gather | solution.py:47
  48.2 4.5 %copy-start.2 = (bf16[768,384]{1,0:T(8,128)(2,1)S(1)}, bf16[768,384]{1,0:T(8,128)(2,1)}, u32[]{:S(2)}) copy-start(bf16[768,384]{1,0:T(8,128)(2,1)} %param.7) | copy-start | bytes 1769476
  48.2 4.3 %collective-permute-start = (bf16[2,512,384]{2,1,0:T(8,128)(2,1)S(1)}, bf16[2,512,384]{2,1,0:T(8,128)(2,1)S(1)}, u32[]{:S(2)}, u32[]{:S(2)}) collective-permute-start(bf16[2,512,384]{2,1,0:T(8,128)(2,1)S(1)} %all_gather.6), channel_id=1, source_target_pairs={{0,1},{1,0},{2,3},{3,2},{4,5},{5,4},{6,7},{7,6},{8,9},{9,8},{10,11... | collective-permute-start | bytes 2359304 | tf_op jit(solution)/shard_map/ppermute | solution.py:34
  160.1 4.2 %collective-permute-start.1 = (f32[512,384]{1,0:T(8,128)S(1)}, f32[512,384]{1,0:T(8,128)S(1)}, u32[]{:S(2)}, u32[]{:S(2)}) collective-permute-start(f32[512,384]{1,0:T(8,128)S(1)} %slice.38), channel_id=1, source_target_pairs={{0,1},{1,0},{2,3},{3,2},{4,5},{5,4},{6,7},{7,6},{8,9},{9,8},{10,11... | collective-permute-start | bytes 2359304 | tf_op jit(solution)/shard_map/ppermute | solution.py:51
  165.1 36.6 %all-to-all-start.1 = ((bf16[16,32,384]{2,1,0:T(8,128)(2,1)}), bf16[16,32,384]{2,1,0:T(8,128)(2,1)S(1)}, u32[]{:S(2)}, u32[]{:S(2)}) async-start(bf16[16,32,384]{2,1,0:T(8,128)(2,1)} %bitcast.9), calls=%async_computation.1 | async-start | bytes 786432 | tf_op jit(solution)/shard_map/all_to_all | solution.py:52
  177.4 3.4 %copy-start.1 = (bf16[2,1024,768]{2,1,0:T(8,128)(2,1)S(1)}, bf16[2,1024,768]{2,1,0:T(8,128)(2,1)}, u32[]{:S(2)}) copy-start(bf16[2,1024,768]{2,1,0:T(8,128)(2,1)} %all-gather.2.cloned.1.call-done) | copy-start | bytes 9437188
Sparse Core Ops, SparseCore 0:
  102.1 55.4 all-gather.1

commit v2 on v1

v2 whole, which is shorter than its diff:
```python
import jax
import jax.numpy as jnp
from jax import lax
from jax.sharding import Mesh
from jax.sharding import PartitionSpec as P

inv_sqrt_two = 0.7071067811865476
inv_sqrt_two_pi = 0.3989422804014327
ROW = ("y", "x")
COL = ("z", "core")
PLANE = ("y", "x", "core")
SWAP = [(0, 1), (1, 0)]
STEPS = (1, 3, 2)
NEAR = (0, 1, -1, 2)
FAR = (0, 4, -4, 8)


def gelu_backward(preact, act_grad):
    normal_cdf = 0.5 * (1.0 + lax.erf(preact * inv_sqrt_two))
    normal_pdf = jnp.exp(-0.5 * preact * preact) * inv_sqrt_two_pi
    activated = (preact * normal_cdf).astype(jnp.bfloat16)
    pre_grad = (act_grad * (normal_cdf + preact * normal_pdf)).astype(jnp.bfloat16)
    return (activated, pre_grad)


def dot(a, b, ca, cb):
    return lax.dot_general(a, b, (((ca,), (cb,)), ((), ())), preferred_element_type=jnp.float32)


def plane_hop(value, axis, step):
    pairs = []
    for y in range(4):
        for x in range(4):
            for core in range(2):
                if core == axis:
                    to = (y, (x + step) % 4)
                else:
                    to = ((y + step) % 4, x)
                pairs.append(((y * 4 + x) * 2 + core, (to[0] * 4 + to[1]) * 2 + core))
    return lax.ppermute(value, PLANE, pairs)


def z_hop(value, step):
    return lax.ppermute(value, "z", [(z, (z + step) % 16) for z in range(16)])


def turn(value, axis, by):
    return lax.dynamic_slice_in_dim(
        jnp.concatenate([value, value], axis=axis), by, value.shape[axis], axis
    )


def body(inputs, cotangent, weight_in, weight_out):
    rows, depth = inputs.shape
    hidden = weight_in.shape[1]
    core = lax.axis_index("core")
    pos_y, pos_x = lax.axis_index("y"), lax.axis_index("x")
    pos_a = jnp.where(core == 0, pos_x, pos_y)
    pos_b = jnp.where(core == 0, pos_y, pos_x)

    both = jnp.stack([inputs, cotangent])
    far = jnp.stack([both] + [z_hop(both, -step) for step in FAR[1:]], axis=1)
    own = jnp.stack([far] + [z_hop(far, -step) for step in NEAR[1:]], axis=1)
    other = lax.ppermute(own, "core", SWAP)
    full = jnp.stack([own, other], axis=1).reshape(2, 4, 4, -1, depth)
    full = turn(turn(full, 1, pos_a), 2, pos_b)
    tokens = full.shape[1] * full.shape[2] * full.shape[3]
    share = full.shape[3]
    x, g = full[0].reshape(tokens, depth), full[1].reshape(tokens, depth)

    pre_part = dot(x, weight_in, 1, 0).astype(jnp.bfloat16).reshape(4, 4 * share, hidden)
    grad_part = dot(g, weight_out, 1, 1).astype(jnp.bfloat16).reshape(4, 4 * share, hidden)
    parts = [jnp.stack([pre_part[d], grad_part[d]]) for d in range(4)]
    landed = [plane_hop(parts[d], 0, d) for d in STEPS]
    sums = parts[0].astype(jnp.float32) + sum(v.astype(jnp.float32) for v in landed)
    sums = sums.reshape(2, 4, share, hidden)
    sums = sums[:, 0] + sum(plane_hop(sums[:, d], 1, d) for d in STEPS)
    hid = jnp.stack(gelu_backward(sums[0], sums[1]))

    line = {0: hid}
    for d in STEPS:
        line[4 - d] = plane_hop(hid, 1, d)
    line = jnp.concatenate([line[d] for d in range(4)], axis=1)
    sheet = {0: line}
    for d in STEPS:
        sheet[4 - d] = plane_hop(line, 0, d)
    sheet = jnp.concatenate([sheet[d] for d in range(4)], axis=1)
    act, pg = sheet[0], sheet[1]

    gi = dot(pg, weight_in, 1, 1).reshape(4, 4, share, depth)
    gi = turn(turn(gi, 0, (4 - pos_a) % 4), 1, (4 - pos_b) % 4).reshape(2, 4, 4, rows, depth)
    chip = gi[0] + lax.ppermute(gi[1], "core", SWAP)
    near = chip.astype(jnp.bfloat16)
    near = chip[0] + sum(
        z_hop(near[j], NEAR[j]).astype(jnp.float32) for j in range(1, 4)
    )
    summed = near[0] + sum(z_hop(near[k], FAR[k]) for k in range(1, 4))
    grad_inputs = summed.astype(jnp.bfloat16)
    grad_weight_out = dot(act, g, 0, 0)
    grad_weight_in = dot(x, pg, 0, 0)
    return (grad_inputs, grad_weight_in, grad_weight_out)


def solution(mesh):
    split = Mesh(mesh.devices.reshape(4, 4, 16, 2), ROW + COL)
    tok, w_in, w_out = P(COL, ROW), P(ROW, COL), P(COL, ROW)
    return jax.shard_map(
        body,
        mesh=split,
        in_specs=(tok, tok, w_in, w_out),
        out_specs=(tok, w_in, w_out),
        check_vma=False,
    )
```

time: 210 us -> 192 us (0.914)
  the two profiles are of different devices: /device:TPU:2 before, /device:TPU:1 now
where the time goes in v2:
time: 192 us; the launch traced here: 191 us
  starting transfers between devices  112 us (58%)
  waiting for transfers between devices  56.8 us (30%)
  local copies, waits for them, and re-layouts  9.15 us (5%)
  matrix products  6.83 us (4%)
  other arithmetic  5.52 us (3%)
    ppermute x12, starting transfers between devices, z_hop(): return lax.ppermute(value, 'z', [(z, (z + step) % 16) for z in range(16)])  60.3 us
    ppermute x12, starting transfers between devices, plane_hop(): return lax.ppermute(value, PLANE, pairs)  39.5 us
    ppermute x12, waiting for transfers between devices, plane_hop(): return lax.ppermute(value, PLANE, pairs)  36.5 us
    ppermute x12, waiting for transfers between devices, z_hop(): return lax.ppermute(value, 'z', [(z, (z + step) % 16) for z in range(16)])  16.5 us
    ppermute x1, starting transfers between devices, body(): chip = gi[0] + lax.ppermute(gi[1], 'core', SWAP)  7.46 us
    dot_general x5, matrix products, dot(): lax.dot_general(a, b, (((ca,), (cb,)), ((), ())), preferred_element_type=...  6.83 us
    unnamed x19, local copies, waits for them, and re-layouts  6.06 us
    ppermute x1, starting transfers between devices, body(): other = lax.ppermute(own, 'core', SWAP)  4.36 us
  transfers between devices with their start and end apart: 26, of which 16 were waited for; matrix products, arithmetic and copies ran while one was open for 5% of the time, Pallas kernels for 0%

profile of v2, /device:TPU:1, one launch (start us, length us, event | category | flops | bytes accessed | tf_op | source)
XLA Modules:
  0.0 191.0 jit_solution(16606152985391253760)
XLA Ops:
  1.5 16.3 %collective-permute-start.2 = (bf16[2,32,384]{2,1,0:T(8,128)(2,1)S(1)}, bf16[2,32,384]{2,1,0:T(8,128)(2,1)S(1)}, u32[]{:S(2)}, u32[]{:S(2)}) collective-permute-start(bf16[2,32,384]{2,1,0:T(8,128)(2,1)S(1)} %get-tuple-element.35), channel_id=1, source_target_pairs={{0,16},{2,18},{4,20},{6,22},{8,24},{10,26},{12,28},{14,30},{16,0},... | collective-permute-start | bytes 147464 | tf_op jit(solution)/shard_map/ppermute | solution.py:44
  17.8 4.0 %collective-permute-start.1 = (bf16[2,32,384]{2,1,0:T(8,128)(2,1)S(1)}, bf16[2,32,384]{2,1,0:T(8,128)(2,1)S(1)}, u32[]{:S(2)}, u32[]{:S(2)}) collective-permute-start(bf16[2,32,384]{2,1,0:T(8,128)(2,1)S(1)} %get-tuple-element.35), channel_id=1, source_target_pairs={{0,8},{2,10},{4,12},{6,14},{8,16},{10,18},{12,20},{14,22},{16,24},... | collective-permute-start | bytes 147464 | tf_op jit(solution)/shard_map/ppermute | solution.py:44
  21.8 5.2 %collective-permute-start = (bf16[2,32,384]{2,1,0:T(8,128)(2,1)S(1)}, bf16[2,32,384]{2,1,0:T(8,128)(2,1)S(1)}, u32[]{:S(2)}, u32[]{:S(2)}) collective-permute-start(bf16[2,32,384]{2,1,0:T(8,128)(2,1)S(1)} %get-tuple-element.35), channel_id=1, source_target_pairs={{0,24},{2,26},{4,28},{6,30},{8,0},{10,2},{12,4},{14,6},{16,8},{18,... | collective-permute-start | bytes 147464 | tf_op jit(solution)/shard_map/ppermute | solution.py:44
  27.2 3.6 %collective-permute-done = bf16[2,32,384]{2,1,0:T(8,128)(2,1)S(1)} collective-permute-done((bf16[2,32,384]{2,1,0:T(8,128)(2,1)S(1)}, bf16[2,32,384]{2,1,0:T(8,128)(2,1)S(1)}, u32[]{:S(2)}, u32[]{:S(2)}) %collective-permute-start) | collective-permute-done | bytes 49184 | tf_op jit(solution)/shard_map/ppermute | solution.py:44
  30.8 4.2 %collective-permute-start.5 = (bf16[2,4,32,384]{3,2,1,0:T(8,128)(2,1)S(1)}, bf16[2,4,32,384]{3,2,1,0:T(8,128)(2,1)S(1)}, u32[]{:S(2)}, u32[]{:S(2)}) collective-permute-start(bf16[2,4,32,384]{3,2,1,0:T(8,128)(2,1)S(1)} %get-tuple-element.33), channel_id=1, source_target_pairs={{0,28},{2,30},{4,0},{6,2},{8,4},{10,6},{12,8},{14,10},{16,12},{18,... | collective-permute-start | bytes 589832 | tf_op jit(solution)/shard_map/ppermute | solution.py:44
  37.8 3.8 %collective-permute-start.3 = (bf16[2,4,32,384]{3,2,1,0:T(8,128)(2,1)S(1)}, bf16[2,4,32,384]{3,2,1,0:T(8,128)(2,1)S(1)}, u32[]{:S(2)}, u32[]{:S(2)}) collective-permute-start(bf16[2,4,32,384]{3,2,1,0:T(8,128)(2,1)S(1)} %get-tuple-element.33), channel_id=1, source_target_pairs={{0,30},{2,0},{4,2},{6,4},{8,6},{10,8},{12,10},{14,12},{16,14},{18,... | collective-permute-start | bytes 589832 | tf_op jit(solution)/shard_map/ppermute | solution.py:44
  42.8 4.5 %collective-permute-done.3 = bf16[2,4,32,384]{3,2,1,0:T(8,128)(2,1)S(1)} collective-permute-done((bf16[2,4,32,384]{3,2,1,0:T(8,128)(2,1)S(1)}, bf16[2,4,32,384]{3,2,1,0:T(8,128)(2,1)S(1)}, u32[]{:S(2)}, u32[]{:S(2)}) %collective-permute-start.3) | collective-permute-done | bytes 196640 | tf_op jit(solution)/shard_map/ppermute | solution.py:44
  47.4 4.4 %collective-permute-start.6 = (bf16[2,4,4,32,384]{4,3,2,1,0:T(8,128)(2,1)S(1)}, bf16[2,4,4,32,384]{4,3,2,1,0:T(8,128)(2,1)S(1)}, u32[]{:S(2)}, u32[]{:S(2)}) collective-permute-start(bf16[2,4,4,32,384]{4,3,2,1,0:T(8,128)(2,1)S(1)} %get-tuple-element.21), channel_id=1, source_target_pairs={{0,1},{1,0},{2,3},{3,2},{4,5},{5,4},{6,7},{7,6},{8,9},{9,8},{10,11... | collective-permute-start | bytes 2359304 | tf_op jit(solution)/shard_map/ppermute | solution.py:64
  58.6 4.8 %collective-permute-start.9 = (bf16[2,256,768]{2,1,0:T(8,128)(2,1)S(1)}, bf16[2,256,768]{2,1,0:T(8,128)(2,1)S(1)}, u32[]{:S(2)}, u32[]{:S(2)}) collective-permute-start(bf16[2,256,768]{2,1,0:T(8,128)(2,1)S(1)} %pad_maximum_fusion.4), channel_id=1, source_target_pairs={{0,64},{1,257},{32,96},{33,289},{64,0},{65,321},{96,32},{97,353},{... | collective-permute-start | bytes 2359304 | tf_op jit(solution)/shard_map/ppermute | solution.py:40
  68.9 4.3 %collective-permute-done.9 = bf16[2,256,768]{2,1,0:T(8,128)(2,1)S(1)} collective-permute-done((bf16[2,256,768]{2,1,0:T(8,128)(2,1)S(1)}, bf16[2,256,768]{2,1,0:T(8,128)(2,1)S(1)}, u32[]{:S(2)}, u32[]{:S(2)}) %collective-permute-start.9) | collective-permute-done | bytes 786464 | tf_op jit(solution)/shard_map/ppermute | solution.py:40
  73.1 8.8 %collective-permute-done.8 = bf16[2,256,768]{2,1,0:T(8,128)(2,1)S(1)} collective-permute-done((bf16[2,256,768]{2,1,0:T(8,128)(2,1)S(1)}, bf16[2,256,768]{2,1,0:T(8,128)(2,1)S(1)}, u32[]{:S(2)}, u32[]{:S(2)}) %collective-permute-start.8) | collective-permute-done | bytes 786464 | tf_op jit(solution)/shard_map/ppermute | solution.py:40
  82.4 4.7 %collective-permute-start.12 = (f32[2,64,768]{2,1,0:T(8,128)S(1)}, f32[2,64,768]{2,1,0:T(8,128)S(1)}, u32[]{:S(2)}, u32[]{:S(2)}) collective-permute-start(f32[2,64,768]{2,1,0:T(8,128)S(1)} %get-tuple-element.9), channel_id=1, source_target_pairs={{0,256},{1,65},{32,288},{33,97},{64,320},{65,1},{96,352},{97,33},{... | collective-permute-start | bytes 1179656 | tf_op jit(solution)/shard_map/ppermute | solution.py:40
  89.3 4.3 %collective-permute-start.11 = (f32[2,64,768]{2,1,0:T(8,128)S(1)}, f32[2,64,768]{2,1,0:T(8,128)S(1)}, u32[]{:S(2)}, u32[]{:S(2)}) collective-permute-start(f32[2,64,768]{2,1,0:T(8,128)S(1)} %get-tuple-element.7), channel_id=1, source_target_pairs={{0,384},{1,97},{32,416},{33,1},{64,448},{65,33},{96,480},{97,65},{... | collective-permute-start | bytes 1179656 | tf_op jit(solution)/shard_map/ppermute | solution.py:40
  93.6 3.5 %collective-permute-done.10 = f32[2,64,768]{2,1,0:T(8,128)S(1)} collective-permute-done((f32[2,64,768]{2,1,0:T(8,128)S(1)}, f32[2,64,768]{2,1,0:T(8,128)S(1)}, u32[]{:S(2)}, u32[]{:S(2)}) %collective-permute-start.10) | collective-permute-done | bytes 393248 | tf_op jit(solution)/shard_map/ppermute | solution.py:40
  99.2 5.0 %collective-permute-start.13 = (bf16[2,64,768]{2,1,0:T(8,128)(2,1)S(1)}, bf16[2,64,768]{2,1,0:T(8,128)(2,1)S(1)}, u32[]{:S(2)}, u32[]{:S(2)}) collective-permute-start(bf16[2,64,768]{2,1,0:T(8,128)(2,1)S(1)} %get-tuple-element.30), channel_id=1, source_target_pairs={{0,384},{1,97},{32,416},{33,1},{64,448},{65,33},{96,480},{97,65},{... | collective-permute-start | bytes 589832 | tf_op jit(solution)/shard_map/ppermute | solution.py:40
  108.7 3.5 %collective-permute-done.14 = bf16[2,64,768]{2,1,0:T(8,128)(2,1)S(1)} collective-permute-done((bf16[2,64,768]{2,1,0:T(8,128)(2,1)S(1)}, bf16[2,64,768]{2,1,0:T(8,128)(2,1)S(1)}, u32[]{:S(2)}, u32[]{:S(2)}) %collective-permute-start.14) | collective-permute-done | bytes 196640 | tf_op jit(solution)/shard_map/ppermute | solution.py:40
  114.6 4.0 %collective-permute-start.16 = (bf16[2,256,768]{2,1,0:T(8,128)(2,1)S(1)}, bf16[2,256,768]{2,1,0:T(8,128)(2,1)}, u32[]{:S(2)}, u32[]{:S(2)}) collective-permute-start(bf16[2,256,768]{2,1,0:T(8,128)(2,1)S(1)} %pad_maximum_fusion.5), channel_id=1, source_target_pairs={{0,96},{1,385},{32,0},{33,417},{64,32},{65,449},{96,64},{97,481},{... | collective-permute-start | bytes 2359304 | tf_op jit(solution)/shard_map/ppermute | solution.py:40
  125.6 10.3 %collective-permute-done.16 = bf16[2,256,768]{2,1,0:T(8,128)(2,1)} collective-permute-done((bf16[2,256,768]{2,1,0:T(8,128)(2,1)S(1)}, bf16[2,256,768]{2,1,0:T(8,128)(2,1)}, u32[]{:S(2)}, u32[]{:S(2)}) %collective-permute-start.16) | collective-permute-done | bytes 786464 | tf_op jit(solution)/shard_map/ppermute | solution.py:40
  145.8 7.5 %collective-permute-start.19 = (f32[4,4,32,384]{3,2,1,0:T(8,128)S(1)}, f32[4,4,32,384]{3,2,1,0:T(8,128)S(1)}, u32[]{:S(2)}, u32[]{:S(2)}) collective-permute-start(f32[4,4,32,384]{3,2,1,0:T(8,128)S(1)} %bitcast.118), channel_id=1, source_target_pairs={{0,1},{1,0},{2,3},{3,2},{4,5},{5,4},{6,7},{7,6},{8,9},{9,8},{10,11... | collective-permute-start | bytes 2359304 | tf_op jit(solution)/shard_map/ppermute | solution.py:92
  157.8 4.3 %collective-permute-start.21 = (bf16[4,32,384]{2,1,0:T(8,128)(2,1)S(1)}, bf16[4,32,384]{2,1,0:T(8,128)(2,1)S(1)}, u32[]{:S(2)}, u32[]{:S(2)}) collective-permute-start(bf16[4,32,384]{2,1,0:T(8,128)(2,1)S(1)} %get-tuple-element.24), channel_id=1, source_target_pairs={{0,30},{2,0},{4,2},{6,4},{8,6},{10,8},{12,10},{14,12},{16,14},{18,... | collective-permute-start | bytes 294920 | tf_op jit(solution)/shard_map/ppermute | solution.py:44
  169.0 5.9 %collective-permute-start.25 = (f32[32,384]{1,0:T(8,128)S(1)}, f32[32,384]{1,0:T(8,128)S(1)}, u32[]{:S(2)}, u32[]{:S(2)}) collective-permute-start(f32[32,384]{1,0:T(8,128)S(1)} %get-tuple-element.28), channel_id=1, source_target_pairs={{0,16},{2,18},{4,20},{6,22},{8,24},{10,26},{12,28},{14,30},{16,0},... | collective-permute-start | bytes 147464 | tf_op jit(solution)/shard_map/ppermute | solution.py:44
  174.9 5.7 %collective-permute-start.23 = (f32[32,384]{1,0:T(8,128)S(1)}, f32[32,384]{1,0:T(8,128)S(1)}, u32[]{:S(2)}, u32[]{:S(2)}) collective-permute-start(f32[32,384]{1,0:T(8,128)S(1)} %get-tuple-element.29), channel_id=1, source_target_pairs={{0,8},{2,10},{4,12},{6,14},{8,16},{10,18},{12,20},{14,22},{16,24},... | collective-permute-start | bytes 147464 | tf_op jit(solution)/shard_map/ppermute | solution.py:44
  180.6 3.5 %collective-permute-start.24 = (f32[32,384]{1,0:T(8,128)S(1)}, f32[32,384]{1,0:T(8,128)S(1)}, u32[]{:S(2)}, u32[]{:S(2)}) collective-permute-start(f32[32,384]{1,0:T(8,128)S(1)} %get-tuple-element.27), channel_id=1, source_target_pairs={{0,24},{2,26},{4,28},{6,30},{8,0},{10,2},{12,4},{14,6},{16,8},{18,... | collective-permute-start | bytes 147464 | tf_op jit(solution)/shard_map/ppermute | solution.py:44
  186.1 4.3 %collective-permute-done.24 = f32[32,384]{1,0:T(8,128)S(1)} collective-permute-done((f32[32,384]{1,0:T(8,128)S(1)}, f32[32,384]{1,0:T(8,128)S(1)}, u32[]{:S(2)}, u32[]{:S(2)}) %collective-permute-start.24) | collective-permute-done | bytes 49184 | tf_op jit(solution)/shard_map/ppermute | solution.py:44
  (79 shorter events, 59.7 us)
Async XLA Ops:
  1.5 25.5 %collective-permute-start.2 = (bf16[2,32,384]{2,1,0:T(8,128)(2,1)S(1)}, bf16[2,32,384]{2,1,0:T(8,128)(2,1)S(1)}, u32[]{:S(2)}, u32[]{:S(2)}) collective-permute-start(bf16[2,32,384]{2,1,0:T(8,128)(2,1)S(1)} %get-tuple-element.35), channel_id=1, source_target_pairs={{0,16},{2,18},{4,20},{6,22},{8,24},{10,26},{12,28},{14,30},{16,0},... | collective-permute-start | bytes 147464 | tf_op jit(solution)/shard_map/ppermute | solution.py:44
  17.8 9.5 %collective-permute-start.1 = (bf16[2,32,384]{2,1,0:T(8,128)(2,1)S(1)}, bf16[2,32,384]{2,1,0:T(8,128)(2,1)S(1)}, u32[]{:S(2)}, u32[]{:S(2)}) collective-permute-start(bf16[2,32,384]{2,1,0:T(8,128)(2,1)S(1)} %get-tuple-element.35), channel_id=1, source_target_pairs={{0,8},{2,10},{4,12},{6,14},{8,16},{10,18},{12,20},{14,22},{16,24},... | collective-permute-start | bytes 147464 | tf_op jit(solution)/shard_map/ppermute | solution.py:44
  21.8 9.0 %collective-permute-start = (bf16[2,32,384]{2,1,0:T(8,128)(2,1)S(1)}, bf16[2,32,384]{2,1,0:T(8,128)(2,1)S(1)}, u32[]{:S(2)}, u32[]{:S(2)}) collective-permute-start(bf16[2,32,384]{2,1,0:T(8,128)(2,1)S(1)} %get-tuple-element.35), channel_id=1, source_target_pairs={{0,24},{2,26},{4,28},{6,30},{8,0},{10,2},{12,4},{14,6},{16,8},{18,... | collective-permute-start | bytes 147464 | tf_op jit(solution)/shard_map/ppermute | solution.py:44
  30.8 10.7 %collective-permute-start.5 = (bf16[2,4,32,384]{3,2,1,0:T(8,128)(2,1)S(1)}, bf16[2,4,32,384]{3,2,1,0:T(8,128)(2,1)S(1)}, u32[]{:S(2)}, u32[]{:S(2)}) collective-permute-start(bf16[2,4,32,384]{3,2,1,0:T(8,128)(2,1)S(1)} %get-tuple-element.33), channel_id=1, source_target_pairs={{0,28},{2,30},{4,0},{6,2},{8,4},{10,6},{12,8},{14,10},{16,12},{18,... | collective-permute-start | bytes 589832 | tf_op jit(solution)/shard_map/ppermute | solution.py:44
  35.0 7.8 %collective-permute-start.4 = (bf16[2,4,32,384]{3,2,1,0:T(8,128)(2,1)S(1)}, bf16[2,4,32,384]{3,2,1,0:T(8,128)(2,1)S(1)}, u32[]{:S(2)}, u32[]{:S(2)}) collective-permute-start(bf16[2,4,32,384]{3,2,1,0:T(8,128)(2,1)S(1)} %get-tuple-element.33), channel_id=1, source_target_pairs={{0,2},{2,4},{4,6},{6,8},{8,10},{10,12},{12,14},{14,16},{16,18},{18... | collective-permute-start | bytes 589832 | tf_op jit(solution)/shard_map/ppermute | solution.py:44
  37.8 9.5 %collective-permute-start.3 = (bf16[2,4,32,384]{3,2,1,0:T(8,128)(2,1)S(1)}, bf16[2,4,32,384]{3,2,1,0:T(8,128)(2,1)S(1)}, u32[]{:S(2)}, u32[]{:S(2)}) collective-permute-start(bf16[2,4,32,384]{3,2,1,0:T(8,128)(2,1)S(1)} %get-tuple-element.33), channel_id=1, source_target_pairs={{0,30},{2,0},{4,2},{6,4},{8,6},{10,8},{12,10},{14,12},{16,14},{18,... | collective-permute-start | bytes 589832 | tf_op jit(solution)/shard_map/ppermute | solution.py:44
  58.6 14.5 %collective-permute-start.9 = (bf16[2,256,768]{2,1,0:T(8,128)(2,1)S(1)}, bf16[2,256,768]{2,1,0:T(8,128)(2,1)S(1)}, u32[]{:S(2)}, u32[]{:S(2)}) collective-permute-start(bf16[2,256,768]{2,1,0:T(8,128)(2,1)S(1)} %pad_maximum_fusion.4), channel_id=1, source_target_pairs={{0,64},{1,257},{32,96},{33,289},{64,0},{65,321},{96,32},{97,353},{... | collective-permute-start | bytes 2359304 | tf_op jit(solution)/shard_map/ppermute | solution.py:40
  63.5 18.4 %collective-permute-start.8 = (bf16[2,256,768]{2,1,0:T(8,128)(2,1)S(1)}, bf16[2,256,768]{2,1,0:T(8,128)(2,1)S(1)}, u32[]{:S(2)}, u32[]{:S(2)}) collective-permute-start(bf16[2,256,768]{2,1,0:T(8,128)(2,1)S(1)} %pad_maximum_fusion.3), channel_id=1, source_target_pairs={{0,96},{1,385},{32,0},{33,417},{64,32},{65,449},{96,64},{97,481},{... | collective-permute-start | bytes 2359304 | tf_op jit(solution)/shard_map/ppermute | solution.py:40
  66.3 15.7 %collective-permute-start.7 = (bf16[2,256,768]{2,1,0:T(8,128)(2,1)S(1)}, bf16[2,256,768]{2,1,0:T(8,128)(2,1)S(1)}, u32[]{:S(2)}, u32[]{:S(2)}) collective-permute-start(bf16[2,256,768]{2,1,0:T(8,128)(2,1)S(1)} %pad_maximum_fusion.2), channel_id=1, source_target_pairs={{0,32},{1,129},{32,64},{33,161},{64,96},{65,193},{96,0},{97,225},{... | collective-permute-start | bytes 2359304 | tf_op jit(solution)/shard_map/ppermute | solution.py:40
  82.4 11.2 %collective-permute-start.12 = (f32[2,64,768]{2,1,0:T(8,128)S(1)}, f32[2,64,768]{2,1,0:T(8,128)S(1)}, u32[]{:S(2)}, u32[]{:S(2)}) collective-permute-start(f32[2,64,768]{2,1,0:T(8,128)S(1)} %get-tuple-element.9), channel_id=1, source_target_pairs={{0,256},{1,65},{32,288},{33,97},{64,320},{65,1},{96,352},{97,33},{... | collective-permute-start | bytes 1179656 | tf_op jit(solution)/shard_map/ppermute | solution.py:40
  87.1 10.0 %collective-permute-start.10 = (f32[2,64,768]{2,1,0:T(8,128)S(1)}, f32[2,64,768]{2,1,0:T(8,128)S(1)}, u32[]{:S(2)}, u32[]{:S(2)}) collective-permute-start(f32[2,64,768]{2,1,0:T(8,128)S(1)} %get-tuple-element.8), channel_id=1, source_target_pairs={{0,128},{1,33},{32,160},{33,65},{64,192},{65,97},{96,224},{97,1},{... | collective-permute-start | bytes 1179656 | tf_op jit(solution)/shard_map/ppermute | solution.py:40
  89.3 9.0 %collective-permute-start.11 = (f32[2,64,768]{2,1,0:T(8,128)S(1)}, f32[2,64,768]{2,1,0:T(8,128)S(1)}, u32[]{:S(2)}, u32[]{:S(2)}) collective-permute-start(f32[2,64,768]{2,1,0:T(8,128)S(1)} %get-tuple-element.7), channel_id=1, source_target_pairs={{0,384},{1,97},{32,416},{33,1},{64,448},{65,33},{96,480},{97,65},{... | collective-permute-start | bytes 1179656 | tf_op jit(solution)/shard_map/ppermute | solution.py:40
  99.2 9.4 %collective-permute-start.13 = (bf16[2,64,768]{2,1,0:T(8,128)(2,1)S(1)}, bf16[2,64,768]{2,1,0:T(8,128)(2,1)S(1)}, u32[]{:S(2)}, u32[]{:S(2)}) collective-permute-start(bf16[2,64,768]{2,1,0:T(8,128)(2,1)S(1)} %get-tuple-element.30), channel_id=1, source_target_pairs={{0,384},{1,97},{32,416},{33,1},{64,448},{65,33},{96,480},{97,65},{... | collective-permute-start | bytes 589832 | tf_op jit(solution)/shard_map/ppermute | solution.py:40
  104.2 8.0 %collective-permute-start.14 = (bf16[2,64,768]{2,1,0:T(8,128)(2,1)S(1)}, bf16[2,64,768]{2,1,0:T(8,128)(2,1)S(1)}, u32[]{:S(2)}, u32[]{:S(2)}) collective-permute-start(bf16[2,64,768]{2,1,0:T(8,128)(2,1)S(1)} %get-tuple-element.30), channel_id=1, source_target_pairs={{0,256},{1,65},{32,288},{33,97},{64,320},{65,1},{96,352},{97,33},{... | collective-permute-start | bytes 589832 | tf_op jit(solution)/shard_map/ppermute | solution.py:40
  106.1 8.4 %collective-permute-start.15 = (bf16[2,64,768]{2,1,0:T(8,128)(2,1)S(1)}, bf16[2,64,768]{2,1,0:T(8,128)(2,1)S(1)}, u32[]{:S(2)}, u32[]{:S(2)}) collective-permute-start(bf16[2,64,768]{2,1,0:T(8,128)(2,1)S(1)} %get-tuple-element.30), channel_id=1, source_target_pairs={{0,128},{1,33},{32,160},{33,65},{64,192},{65,97},{96,224},{97,1},{... | collective-permute-start | bytes 589832 | tf_op jit(solution)/shard_map/ppermute | solution.py:40
  114.6 21.3 %collective-permute-start.16 = (bf16[2,256,768]{2,1,0:T(8,128)(2,1)S(1)}, bf16[2,256,768]{2,1,0:T(8,128)(2,1)}, u32[]{:S(2)}, u32[]{:S(2)}) collective-permute-start(bf16[2,256,768]{2,1,0:T(8,128)(2,1)S(1)} %pad_maximum_fusion.5), channel_id=1, source_target_pairs={{0,96},{1,385},{32,0},{33,417},{64,32},{65,449},{96,64},{97,481},{... | collective-permute-start | bytes 2359304 | tf_op jit(solution)/shard_map/ppermute | solution.py:40
  118.6 19.5 %collective-permute-start.17 = (bf16[2,256,768]{2,1,0:T(8,128)(2,1)S(1)}, bf16[2,256,768]{2,1,0:T(8,128)(2,1)S(1)}, u32[]{:S(2)}, u32[]{:S(2)}) collective-permute-start(bf16[2,256,768]{2,1,0:T(8,128)(2,1)S(1)} %pad_maximum_fusion.5), channel_id=1, source_target_pairs={{0,64},{1,257},{32,96},{33,289},{64,0},{65,321},{96,32},{97,353},{... | collective-permute-start | bytes 2359304 | tf_op jit(solution)/shard_map/ppermute | solution.py:40
  121.0 20.5 %collective-permute-start.18 = (bf16[2,256,768]{2,1,0:T(8,128)(2,1)S(1)}, bf16[2,256,768]{2,1,0:T(8,128)(2,1)S(1)}, u32[]{:S(2)}, u32[]{:S(2)}) collective-permute-start(bf16[2,256,768]{2,1,0:T(8,128)(2,1)S(1)} %pad_maximum_fusion.5), channel_id=1, source_target_pairs={{0,32},{1,129},{32,64},{33,161},{64,96},{65,193},{96,0},{97,225},{... | collective-permute-start | bytes 2359304 | tf_op jit(solution)/shard_map/ppermute | solution.py:40
  145.8 9.4 %collective-permute-start.19 = (f32[4,4,32,384]{3,2,1,0:T(8,128)S(1)}, f32[4,4,32,384]{3,2,1,0:T(8,128)S(1)}, u32[]{:S(2)}, u32[]{:S(2)}) collective-permute-start(f32[4,4,32,384]{3,2,1,0:T(8,128)S(1)} %bitcast.118), channel_id=1, source_target_pairs={{0,1},{1,0},{2,3},{3,2},{4,5},{5,4},{6,7},{7,6},{8,9},{9,8},{10,11... | collective-permute-start | bytes 2359304 | tf_op jit(solution)/shard_map/ppermute | solution.py:92
  155.3 11.0 %collective-permute-start.22 = (bf16[4,32,384]{2,1,0:T(8,128)(2,1)S(1)}, bf16[4,32,384]{2,1,0:T(8,128)(2,1)S(1)}, u32[]{:S(2)}, u32[]{:S(2)}) collective-permute-start(bf16[4,32,384]{2,1,0:T(8,128)(2,1)S(1)} %get-tuple-element.23), channel_id=1, source_target_pairs={{0,4},{2,6},{4,8},{6,10},{8,12},{10,14},{12,16},{14,18},{16,20},{1... | collective-permute-start | bytes 294920 | tf_op jit(solution)/shard_map/ppermute | solution.py:44
  157.8 8.4 %collective-permute-start.21 = (bf16[4,32,384]{2,1,0:T(8,128)(2,1)S(1)}, bf16[4,32,384]{2,1,0:T(8,128)(2,1)S(1)}, u32[]{:S(2)}, u32[]{:S(2)}) collective-permute-start(bf16[4,32,384]{2,1,0:T(8,128)(2,1)S(1)} %get-tuple-element.24), channel_id=1, source_target_pairs={{0,30},{2,0},{4,2},{6,4},{8,6},{10,8},{12,10},{14,12},{16,14},{18,... | collective-permute-start | bytes 294920 | tf_op jit(solution)/shard_map/ppermute | solution.py:44
  169.0 17.1 %collective-permute-start.25 = (f32[32,384]{1,0:T(8,128)S(1)}, f32[32,384]{1,0:T(8,128)S(1)}, u32[]{:S(2)}, u32[]{:S(2)}) collective-permute-start(f32[32,384]{1,0:T(8,128)S(1)} %get-tuple-element.28), channel_id=1, source_target_pairs={{0,16},{2,18},{4,20},{6,22},{8,24},{10,26},{12,28},{14,30},{16,0},... | collective-permute-start | bytes 147464 | tf_op jit(solution)/shard_map/ppermute | solution.py:44
  174.9 11.2 %collective-permute-start.23 = (f32[32,384]{1,0:T(8,128)S(1)}, f32[32,384]{1,0:T(8,128)S(1)}, u32[]{:S(2)}, u32[]{:S(2)}) collective-permute-start(f32[32,384]{1,0:T(8,128)S(1)} %get-tuple-element.29), channel_id=1, source_target_pairs={{0,8},{2,10},{4,12},{6,14},{8,16},{10,18},{12,20},{14,22},{16,24},... | collective-permute-start | bytes 147464 | tf_op jit(solution)/shard_map/ppermute | solution.py:44
  180.6 9.8 %collective-permute-start.24 = (f32[32,384]{1,0:T(8,128)S(1)}, f32[32,384]{1,0:T(8,128)S(1)}, u32[]{:S(2)}, u32[]{:S(2)}) collective-permute-start(f32[32,384]{1,0:T(8,128)S(1)} %get-tuple-element.27), channel_id=1, source_target_pairs={{0,24},{2,26},{4,28},{6,30},{8,0},{10,2},{12,4},{14,6},{16,8},{18,... | collective-permute-start | bytes 147464 | tf_op jit(solution)/shard_map/ppermute | solution.py:44
  (9 other events, 124.4 us)

commit v3 on v1

v3 whole, which is shorter than its diff:
```python
import jax
import jax.numpy as jnp
from jax import lax
from jax.sharding import Mesh
from jax.sharding import PartitionSpec as P

inv_sqrt_two = 0.7071067811865476
inv_sqrt_two_pi = 0.3989422804014327
ROW = ("y", "x")
COL = ("z", "core")
PLANE = ("y", "x", "core")
SWAP = [(0, 1), (1, 0)]


def gelu_backward(preact, act_grad):
    normal_cdf = 0.5 * (1.0 + lax.erf(preact * inv_sqrt_two))
    normal_pdf = jnp.exp(-0.5 * preact * preact) * inv_sqrt_two_pi
    activated = (preact * normal_cdf).astype(jnp.bfloat16)
    pre_grad = (act_grad * (normal_cdf + preact * normal_pdf)).astype(jnp.bfloat16)
    return (activated, pre_grad)


def dot(a, b, ca, cb):
    return lax.dot_general(a, b, (((ca,), (cb,)), ((), ())), preferred_element_type=jnp.float32)


def device_in_plane(y, x, core):
    return (y * 4 + x) * 2 + core


def rings(axis):
    groups = []
    for core in range(2):
        for i in range(4):
            if core == axis:
                groups.append([device_in_plane(i, j, core) for j in range(4)])
            else:
                groups.append([device_in_plane(j, i, core) for j in range(4)])
    return groups


def swap_blocks(value, axis):
    return lax.all_to_all(value, PLANE, 0, 0, tiled=True, axis_index_groups=rings(axis))


def gather_ring(value, axis):
    return lax.all_gather(value, PLANE, axis=0, axis_index_groups=rings(axis))


def add_blocks(value):
    total = value[0].astype(jnp.float32)
    for i in range(1, value.shape[0]):
        total = total + value[i].astype(jnp.float32)
    return total


def gather_row(value):
    line = gather_ring(value, 1)
    sheet = swap_blocks(jnp.broadcast_to(line[None], (4,) + line.shape), 0)
    return sheet.reshape(-1, value.shape[-1])


def body(inputs, cotangent, weight_in, weight_out):
    rows, depth = inputs.shape
    hidden = weight_in.shape[1]
    own = lax.all_gather(jnp.stack([inputs, cotangent]), "z", axis=0)
    other = lax.ppermute(own, "core", SWAP)
    x = jnp.concatenate([own[:, 0], other[:, 0]]).reshape(-1, depth)
    g = jnp.concatenate([own[:, 1], other[:, 1]]).reshape(-1, depth)
    share = x.shape[0] // 16

    pre_part = dot(x, weight_in, 1, 0).astype(jnp.bfloat16).reshape(4, 4, share, hidden)
    grad_part = dot(g, weight_out, 1, 1).astype(jnp.bfloat16).reshape(4, 4, share, hidden)
    line = add_blocks(swap_blocks(jnp.stack([pre_part, grad_part], axis=2), 0))
    sums = add_blocks(swap_blocks(line, 1))
    activated, pre_grad = gelu_backward(sums[0], sums[1])

    pg = gather_row(pre_grad)
    gi = dot(pg, weight_in, 1, 1).reshape(2, 16, rows, depth)
    chip = gi[0] + lax.ppermute(gi[1], "core", SWAP)
    pieces, activated = lax.optimization_barrier((chip.astype(jnp.bfloat16), activated))
    pieces = lax.all_to_all(pieces, "z", 0, 0, tiled=True)
    act = gather_row(activated)
    grad_weight_in = dot(x, pg, 0, 0)
    grad_weight_out = dot(act, g, 0, 0)
    grad_inputs = add_blocks(pieces).astype(jnp.bfloat16)
    return (grad_inputs, grad_weight_in, grad_weight_out)


def solution(mesh):
    split = Mesh(mesh.devices.reshape(4, 4, 16, 2), ROW + COL)
    tok, w_in, w_out = P(COL, ROW), P(ROW, COL), P(COL, ROW)
    return jax.shard_map(
        body,
        mesh=split,
        in_specs=(tok, tok, w_in, w_out),
        out_specs=(tok, w_in, w_out),
        check_vma=False,
    )
```

time: 210 us -> 187 us (0.89)
  the two profiles are of different devices: /device:TPU:2 before, /device:TPU:32 now
where the time goes in v3:
time: 187 us; the launch traced here: 186 us
  blocking collectives  140 us (75%)
  waiting for transfers between devices  20.7 us (11%)
  starting transfers between devices  13 us (7%)
  matrix products  6.82 us (4%)
  other arithmetic  3.38 us (2%)
    all_to_all x4, blocking collectives, swap_blocks(): lax.all_to_all(value, PLANE, 0, 0, tiled=True, axis_index_groups=rings(ax...  77.2 us
    all_gather x1, blocking collectives, body(): own = lax.all_gather(jnp.stack([inputs, cotangent]), 'z', axis=0)  37.7 us
    all_gather x2, blocking collectives, gather_ring(): return lax.all_gather(value, PLANE, axis=0, axis_index_groups=rings(axis))  25 us
    all_to_all x1, waiting for transfers between devices, body(): pieces = lax.all_to_all(pieces, 'z', 0, 0, tiled=True)  16.3 us
    all_to_all x1, starting transfers between devices, body(): pieces = lax.all_to_all(pieces, 'z', 0, 0, tiled=True)  9.11 us
    dot_general x5, matrix products, dot(): lax.dot_general(a, b, (((ca,), (cb,)), ((), ())), preferred_element_type=...  6.82 us
  transfers between devices with their start and end apart: 3, of which 3 were waited for; matrix products, arithmetic and copies ran while one was open for 2% of the time, Pallas kernels for 0%

profile of v3, /device:TPU:32, one launch (start us, length us, event | category | flops | bytes accessed | tf_op | source)
XLA Modules:
  0.0 186.2 jit_solution(7796209791416420072)
XLA Ops:
  0.6 0.8 pad_maximum_fusion.3
  1.5 37.7 %all-gather = bf16[32,32,384]{2,1,0:T(8,128)(2,1)S(1)} all-gather(bf16[2,32,384]{2,1,0:T(8,128)(2,1)S(1)} %pad_maximum_fusion.3), channel_id=2, replica_groups=mesh['y'=4,'x'=4,'z'=16,'core'=2] {'z'}, dimensions={0}, use_global_device_ids=true | all-gather | bytes 835584 | tf_op jit(solution)/shard_map/all_gather | solution.py:66
  39.2 1.9 %collective-permute-start = (bf16[16,2,32,384]{3,2,0,1:T(8,128)(2,1)S(1)}, bf16[16,2,32,384]{3,2,0,1:T(8,128)(2,1)S(1)}, u32[]{:S(2)}, u32[]{:S(2)}) collective-permute-start(bf16[16,2,32,384]{3,2,0,1:T(8,128)(2,1)S(1)} %copy.10), channel_id=1, source_target_pairs={{0,1},{1,0},{2,3},{3,2},{4,5},{5,4},{6,7},{7,6},{8,9},{9,8},{10,11... | collective-permute-start | bytes 2359304 | tf_op jit(solution)/shard_map/ppermute | solution.py:67
  41.3 2.1 %collective-permute-done = bf16[16,2,32,384]{3,2,0,1:T(8,128)(2,1)S(1)} collective-permute-done((bf16[16,2,32,384]{3,2,0,1:T(8,128)(2,1)S(1)}, bf16[16,2,32,384]{3,2,0,1:T(8,128)(2,1)S(1)}, u32[]{:S(2)}, u32[]{:S(2)}) %collective-permute-start) | collective-permute-done | bytes 786464 | tf_op jit(solution)/shard_map/ppermute | solution.py:67
  43.7 0.9 copy-done.4
  44.6 1.0 convolution_convert_fusion
  45.6 1.0 convolution_convert_fusion.1
  46.6 0.3 pad_maximum_fusion
  46.9 26.2 %all_to_all.25 = bf16[4,4,2,64,768]{4,3,1,2,0:T(8,128)(2,1)S(1)} all-to-all(bf16[4,4,2,64,768]{4,3,1,2,0:T(8,128)(2,1)S(1)} %pad_maximum_fusion), channel_id=1, replica_groups={{0,32,64,96},{128,160,192,224},{256,288,320,352},{384,416,448,480},{1,1..., dimensions={0} | all-to-all | bytes 6291456 | tf_op jit(solution)/shard_map/all_to_all | solution.py:43
  73.1 0.4 add_bitcast_fusion
  73.6 18.0 %all_to_all.26 = f32[4,2,64,768]{3,2,1,0:T(8,128)S(1)} all-to-all(f32[4,2,64,768]{3,2,1,0:T(8,128)S(1)} %copy.14), channel_id=1, replica_groups={{0,128,256,384},{32,160,288,416},{64,192,320,448},{96,224,352,480},{1,3..., dimensions={0} | all-to-all | bytes 3145728 | tf_op jit(solution)/shard_map/all_to_all | solution.py:43
  91.7 12.5 %all_gather.18 = bf16[4,64,768]{2,1,0:T(8,128)(2,1)S(1)} all-gather(bf16[1,64,768]{2,1,0:T(8,128)(2,1)S(1)} %fusion.5), channel_id=1, replica_groups={{0,128,256,384},{32,160,288,416},{64,192,320,448},{96,224,352,480},{1,3..., dimensions={0}, use_global_device_ids=true | all-gather | bytes 491520 | tf_op jit(solution)/shard_map/all_gather | solution.py:47
  104.4 16.1 %all_to_all.27 = bf16[4,4,64,768]{3,2,1,0:T(8,128)(2,1)S(1)} all-to-all(bf16[4,4,64,768]{3,2,1,0:T(8,128)(2,1)S(1)} %broadcast_in_dim.4), channel_id=1, replica_groups={{0,32,64,96},{128,160,192,224},{256,288,320,352},{384,416,448,480},{1,1..., dimensions={0} | all-to-all | bytes 3145728 | tf_op jit(solution)/shard_map/all_to_all | solution.py:43
  120.6 1.0 fusion.15
  121.7 1.9 %collective-permute-start.1 = (f32[16,32,384]{2,1,0:T(8,128)S(1)}, f32[16,32,384]{2,1,0:T(8,128)S(1)}, u32[]{:S(2)}, u32[]{:S(2)}) collective-permute-start(f32[16,32,384]{2,1,0:T(8,128)S(1)} %bitcast.85), channel_id=1, source_target_pairs={{0,1},{1,0},{2,3},{3,2},{4,5},{5,4},{6,7},{7,6},{8,9},{9,8},{10,11... | collective-permute-start | bytes 2359304 | tf_op jit(solution)/shard_map/ppermute | solution.py:80
  123.7 2.2 %collective-permute-done.1 = f32[16,32,384]{2,1,0:T(8,128)S(1)} collective-permute-done((f32[16,32,384]{2,1,0:T(8,128)S(1)}, f32[16,32,384]{2,1,0:T(8,128)S(1)}, u32[]{:S(2)}, u32[]{:S(2)}) %collective-permute-start.1) | collective-permute-done | bytes 786464 | tf_op jit(solution)/shard_map/ppermute | solution.py:80
  125.9 0.8 add_convert_fusion
  126.7 12.5 %all-gather.1 = bf16[256,768]{1,0:T(8,128)(2,1)S(1)} all-gather(bf16[64,768]{1,0:T(8,128)(2,1)S(1)} %fusion.12), channel_id=3, replica_groups={{0,128,256,384},{32,160,288,416},{64,192,320,448},{96,224,352,480},{1,3..., dimensions={0}, use_global_device_ids=true | all-gather | bytes 491520 | tf_op jit(solution)/shard_map/all_gather | solution.py:47
  139.4 16.9 %all_to_all.28 = bf16[4,4,64,768]{3,2,1,0:T(8,128)(2,1)} all-to-all(bf16[4,4,64,768]{3,2,1,0:T(8,128)(2,1)S(1)} %broadcast_in_dim.5), channel_id=1, replica_groups={{0,32,64,96},{128,160,192,224},{256,288,320,352},{384,416,448,480},{1,1..., dimensions={0} | all-to-all | bytes 3145728 | tf_op jit(solution)/shard_map/all_to_all | solution.py:43
  156.2 9.1 %all-to-all-start.3 = ((bf16[16,32,384]{2,1,0:T(8,128)(2,1)}), bf16[16,32,384]{2,1,0:T(8,128)(2,1)S(1)}, u32[]{:S(2)}, u32[]{:S(2)}) async-start(bf16[16,32,384]{2,1,0:T(8,128)(2,1)} %add_convert_fusion), calls=%async_computation.3 | async-start | bytes 786432 | tf_op jit(solution)/shard_map/all_to_all | solution.py:82
  165.4 1.8 fusion.16
  167.2 2.0 %fusion.17 = f32[768,384]{1,0:T(8,128)} fusion(bf16[1024,768]{1,0:T(8,128)(2,1)S(1)} %bitcast.79, bf16[1024,384]{1,0:T(8,128)(2,1)S(1)} %bitcast.84), kind=kOutput, calls=%fused_computation.39 | convolution fusion | flops 603979776 | bytes 3538944 | tf_op jit(solution)/shard_map/dot_general | solution.py:24
  169.2 16.3 %all-to-all-done.3 = bf16[16,32,384]{2,1,0:T(8,128)(2,1)S(1)} async-done(((bf16[16,32,384]{2,1,0:T(8,128)(2,1)}), bf16[16,32,384]{2,1,0:T(8,128)(2,1)S(1)}, u32[]{:S(2)}, u32[]{:S(2)}) %all-to-all-start.3) | async-done | bytes 393248 | tf_op jit(solution)/shard_map/all_to_all | solution.py:82
  185.5 0.7 fusion.13
  (21 shorter events, 1.2 us)
Async XLA Ops:
  0.6 45.0 %copy-start = (bf16[384,768]{1,0:T(8,128)(2,1)S(1)}, bf16[384,768]{1,0:T(8,128)(2,1)}, u32[]{:S(2)}) copy-start(bf16[384,768]{1,0:T(8,128)(2,1)} %param.6) | copy-start | bytes 1769476
  39.2 4.2 %collective-permute-start = (bf16[16,2,32,384]{3,2,0,1:T(8,128)(2,1)S(1)}, bf16[16,2,32,384]{3,2,0,1:T(8,128)(2,1)S(1)}, u32[]{:S(2)}, u32[]{:S(2)}) collective-permute-start(bf16[16,2,32,384]{3,2,0,1:T(8,128)(2,1)S(1)} %copy.10), channel_id=1, source_target_pairs={{0,1},{1,0},{2,3},{3,2},{4,5},{5,4},{6,7},{7,6},{8,9},{9,8},{10,11... | collective-permute-start | bytes 2359304 | tf_op jit(solution)/shard_map/ppermute | solution.py:67
  43.5 1.1 copy-start.4
  43.7 2.9 %copy-start.2 = (bf16[32,32,384]{2,1,0:T(8,128)(2,1)}, bf16[32,32,384]{2,1,0:T(8,128)(2,1)S(1)}, u32[]{:S(2)}) copy-start(bf16[32,32,384]{2,1,0:T(8,128)(2,1)S(1)} %get-tuple-element.12) | copy-start | bytes 2359300
  121.7 4.2 %collective-permute-start.1 = (f32[16,32,384]{2,1,0:T(8,128)S(1)}, f32[16,32,384]{2,1,0:T(8,128)S(1)}, u32[]{:S(2)}, u32[]{:S(2)}) collective-permute-start(f32[16,32,384]{2,1,0:T(8,128)S(1)} %bitcast.85), channel_id=1, source_target_pairs={{0,1},{1,0},{2,3},{3,2},{4,5},{5,4},{6,7},{7,6},{8,9},{9,8},{10,11... | collective-permute-start | bytes 2359304 | tf_op jit(solution)/shard_map/ppermute | solution.py:80
  156.2 29.3 %all-to-all-start.3 = ((bf16[16,32,384]{2,1,0:T(8,128)(2,1)}), bf16[16,32,384]{2,1,0:T(8,128)(2,1)S(1)}, u32[]{:S(2)}, u32[]{:S(2)}) async-start(bf16[16,32,384]{2,1,0:T(8,128)(2,1)} %add_convert_fusion), calls=%async_computation.3 | async-start | bytes 786432 | tf_op jit(solution)/shard_map/all_to_all | solution.py:82
  165.3 1.8 copy-start.1
  165.4 1.8 copy-start.3

commit v4 on v3

v4 whole, which is shorter than its diff:
```python
import jax
import jax.numpy as jnp
from jax import lax
from jax.sharding import Mesh
from jax.sharding import PartitionSpec as P

inv_sqrt_two = 0.7071067811865476
inv_sqrt_two_pi = 0.3989422804014327
ROW = ("y", "x")
COL = ("z", "core")
SWAP = [(0, 1), (1, 0)]


def gelu_backward(preact, act_grad):
    normal_cdf = 0.5 * (1.0 + lax.erf(preact * inv_sqrt_two))
    normal_pdf = jnp.exp(-0.5 * preact * preact) * inv_sqrt_two_pi
    activated = (preact * normal_cdf).astype(jnp.bfloat16)
    pre_grad = (act_grad * (normal_cdf + preact * normal_pdf)).astype(jnp.bfloat16)
    return (activated, pre_grad)


def dot(a, b, ca, cb):
    return lax.dot_general(a, b, (((ca,), (cb,)), ((), ())), preferred_element_type=jnp.float32)


def add_blocks(value):
    total = value[0].astype(jnp.float32)
    for i in range(1, value.shape[0]):
        total = total + value[i].astype(jnp.float32)
    return total


def body(inputs, cotangent, weight_in, weight_out):
    rows, depth = inputs.shape
    hidden = weight_in.shape[1]
    own = lax.all_gather(jnp.stack([inputs, cotangent]), "z", axis=0)
    other = lax.ppermute(own, "core", SWAP)
    x = jnp.concatenate([own[:, 0], other[:, 0]]).reshape(-1, depth)
    g = jnp.concatenate([own[:, 1], other[:, 1]]).reshape(-1, depth)
    share = x.shape[0] // 16

    pre_part = dot(x, weight_in, 1, 0)
    preact = lax.psum_scatter(pre_part, ROW, scatter_dimension=0, tiled=True)
    grad_part = dot(g, weight_out, 1, 1).astype(jnp.bfloat16).reshape(16, share, hidden)
    act_grad = add_blocks(lax.all_to_all(grad_part, ROW, 0, 0, tiled=True))
    activated, pre_grad = gelu_backward(preact, act_grad)

    act = lax.all_gather(activated, ROW, axis=0, tiled=True)
    copies = jnp.broadcast_to(pre_grad[None], (16, share, hidden))
    pg = lax.all_to_all(copies, ROW, 0, 0, tiled=True).reshape(-1, hidden)
    gi = dot(pg, weight_in, 1, 1).reshape(2, 16, rows, depth)
    chip = gi[0] + lax.ppermute(gi[1], "core", SWAP)
    pieces = lax.all_to_all(chip.astype(jnp.bfloat16), "z", 0, 0, tiled=True)
    grad_weight_in = dot(x, pg, 0, 0)
    grad_weight_out = dot(act, g, 0, 0)
    grad_inputs = add_blocks(pieces).astype(jnp.bfloat16)
    return (grad_inputs, grad_weight_in, grad_weight_out)


def solution(mesh):
    split = Mesh(mesh.devices.reshape(4, 4, 16, 2), ROW + COL)
    tok, w_in, w_out = P(COL, ROW), P(ROW, COL), P(COL, ROW)
    return jax.shard_map(
        body,
        mesh=split,
        in_specs=(tok, tok, w_in, w_out),
        out_specs=(tok, w_in, w_out),
        check_vma=False,
    )
```

time: 187 us -> 232 us (1.24)
  the two profiles are of different devices: /device:TPU:32 before, /device:TPU:1 now
where the time goes in v4:
time: 232 us; the launch traced here: 231 us
  waiting for transfers between devices  102 us (44%)
  blocking collectives  65.6 us (28%)
  starting transfers between devices  32.8 us (14%)
  between operations  14.2 us (6%)
  matrix products  10.1 us (4%)
  other arithmetic  4.35 us (2%)
  local copies, waits for them, and re-layouts  2.56 us (1%)
    reduce_scatter x1, waiting for transfers between devices, body(): preact = lax.psum_scatter(pre_part, ROW, scatter_dimension=0, tiled=True)  55.6 us
    all_gather x1, blocking collectives, body(): own = lax.all_gather(jnp.stack([inputs, cotangent]), 'z', axis=0)  33.9 us
    all_to_all x1, blocking collectives, body(): act_grad = add_blocks(lax.all_to_all(grad_part, ROW, 0, 0, tiled=True))  31.7 us
    all_gather x1, waiting for transfers between devices, body(): act = lax.all_gather(activated, ROW, axis=0, tiled=True)  22.4 us
    all_to_all x1, waiting for transfers between devices, body(): pg = lax.all_to_all(copies, ROW, 0, 0, tiled=True).reshape(-1, hidden)  19.1 us
    all_to_all x1, starting transfers between devices, body(): pieces = lax.all_to_all(chip.astype(jnp.bfloat16), 'z', 0, 0, tiled=True)  12 us
    dot_general x5, matrix products, dot(): lax.dot_general(a, b, (((ca,), (cb,)), ((), ())), preferred_element_type=...  10.1 us
    ppermute x1, starting transfers between devices, body(): other = lax.ppermute(own, 'core', SWAP)  9.64 us
  transfers between devices with their start and end apart: 6, of which 5 were waited for; matrix products, arithmetic and copies ran while one was open for 4% of the time, Pallas kernels for 0%

profile of v4, /device:TPU:1, one launch (start us, length us, event | category | flops | bytes accessed | tf_op | source)
XLA Modules:
  0.0 231.1 jit_solution(8164465835545325983)
XLA Ops:
  7.2 0.8 pad_maximum_fusion.2
  8.0 33.9 %all-gather = bf16[32,32,384]{2,1,0:T(8,128)(2,1)S(1)} all-gather(bf16[2,32,384]{2,1,0:T(8,128)(2,1)S(1)} %pad_maximum_fusion.2), channel_id=2, replica_groups=mesh['y'=4,'x'=4,'z'=16,'core'=2] {'z'}, dimensions={0}, use_global_device_ids=true | all-gather | bytes 835584 | tf_op jit(solution)/shard_map/all_gather | solution.py:36
  42.0 9.6 %collective-permute-start = (bf16[16,2,32,384]{3,2,0,1:T(8,128)(2,1)S(1)}, bf16[16,2,32,384]{3,2,0,1:T(8,128)(2,1)S(1)}, u32[]{:S(2)}, u32[]{:S(2)}) collective-permute-start(bf16[16,2,32,384]{3,2,0,1:T(8,128)(2,1)S(1)} %copy.9), channel_id=1, source_target_pairs={{0,1},{1,0},{2,3},{3,2},{4,5},{5,4},{6,7},{7,6},{8,9},{9,8},{10,11... | collective-permute-start | bytes 2359304 | tf_op jit(solution)/shard_map/ppermute | solution.py:37
  51.7 1.8 collective-permute-done
  53.8 2.6 %fusion.8 = f32[1024,768]{1,0:T(8,128)} fusion(bf16[1024,384]{1,0:T(8,128)(2,1)S(1)} %bitcast.46, bf16[384,768]{1,0:T(8,128)(2,1)S(1)} %copy-done), kind=kOutput, calls=%fused_computation.24 | convolution fusion | flops 603979776 | bytes 4521984 | tf_op jit(solution)/shard_map/dot_general | solution.py:23
  56.6 0.9 copy-done.2
  57.5 1.0 convolution_convert_fusion
  58.5 31.7 %all_to_all.15 = bf16[16,64,768]{2,1,0:T(8,128)(2,1)S(1)} all-to-all(bf16[16,64,768]{2,1,0:T(8,128)(2,1)S(1)} %bitcast.49), channel_id=1, replica_groups=mesh['y'=4,'x'=4,'z'=16,'core'=2] {'y','x'}, dimensions={0} | all-to-all | bytes 3145728 | tf_op jit(solution)/shard_map/all_to_all | solution.py:45
  90.2 55.6 %reduce-scatter.2.cloned.1.call-done = f32[64,768]{1,0:T(8,128)} async-done(((f32[1024,768]{1,0:T(8,128)}), f32[64,768]{1,0:T(8,128)}) %reduce-scatter.2.cloned.1.call-update) | async-done | bytes 196624 | tf_op jit(solution)/shard_map/reduce_scatter | solution.py:43
  145.8 1.9 multiply_convert_fusion
  147.6 1.3 broadcast_in_dim.2
  148.9 4.4 %all-to-all-start.1 = ((bf16[16,64,768]{2,1,0:T(8,128)(2,1)}), bf16[16,64,768]{2,1,0:T(8,128)(2,1)S(1)}, u32[]{:S(2)}, u32[]{:S(2)}) async-start(bf16[16,64,768]{2,1,0:T(8,128)(2,1)} %broadcast_in_dim.2), calls=%async_computation.2 | async-start | bytes 3145728 | tf_op jit(solution)/shard_map/all_to_all | solution.py:50
  153.4 0.7 all-gather.3.cloned.1.call-update
  154.1 19.1 %all-to-all-done.1 = bf16[16,64,768]{2,1,0:T(8,128)(2,1)S(1)} async-done(((bf16[16,64,768]{2,1,0:T(8,128)(2,1)}), bf16[16,64,768]{2,1,0:T(8,128)(2,1)S(1)}, u32[]{:S(2)}, u32[]{:S(2)}) %all-to-all-start.1) | async-done | bytes 1572896 | tf_op jit(solution)/shard_map/all_to_all | solution.py:50
  173.2 1.0 fusion.9
  174.2 0.1 fusion.7
  174.3 6.7 %collective-permute-start.1 = (f32[16,32,384]{2,1,0:T(8,128)S(1)}, f32[16,32,384]{2,1,0:T(8,128)S(1)}, u32[]{:S(2)}, u32[]{:S(2)}) collective-permute-start(f32[16,32,384]{2,1,0:T(8,128)S(1)} %bitcast.52), channel_id=1, source_target_pairs={{0,1},{1,0},{2,3},{3,2},{4,5},{5,4},{6,7},{7,6},{8,9},{9,8},{10,11... | collective-permute-start | bytes 2359304 | tf_op jit(solution)/shard_map/ppermute | solution.py:52
  181.0 1.9 collective-permute-done.1
  182.9 0.8 add_convert_fusion
  183.7 12.0 %all-to-all-start.2 = ((bf16[16,32,384]{2,1,0:T(8,128)(2,1)}), bf16[16,32,384]{2,1,0:T(8,128)(2,1)S(1)}, u32[]{:S(2)}, u32[]{:S(2)}) async-start(bf16[16,32,384]{2,1,0:T(8,128)(2,1)} %add_convert_fusion), calls=%async_computation.3 | async-start | bytes 786432 | tf_op jit(solution)/shard_map/all_to_all | solution.py:53
  195.7 1.8 fusion.10
  197.5 22.4 %all-gather.3.cloned.1.call-done = bf16[1024,768]{1,0:T(8,128)(2,1)} async-done(((bf16[64,768]{1,0:T(8,128)(2,1)}), bf16[1024,768]{1,0:T(8,128)(2,1)}) %all-gather.3.cloned.1.call-update) | async-done | bytes 1572880 | tf_op jit(solution)/shard_map/all_gather | solution.py:48
  220.0 3.6 %fusion.11 = f32[768,384]{1,0:T(8,128)} fusion(bf16[1024,768]{1,0:T(8,128)(2,1)} %all-gather.3.cloned.1.call-done, bf16[1024,384]{1,0:T(8,128)(2,1)} %bitcast.51), kind=kOutput, calls=%fused_computation.27 | convolution fusion | flops 603979776 | bytes 3538944 | tf_op jit(solution)/shard_map/dot_general | solution.py:23
  223.6 0.7 fusion.6
  (15 shorter events, 0.5 us)
Async XLA Ops:
  7.2 46.6 %copy-start = (bf16[384,768]{1,0:T(8,128)(2,1)S(1)}, bf16[384,768]{1,0:T(8,128)(2,1)}, u32[]{:S(2)}) copy-start(bf16[384,768]{1,0:T(8,128)(2,1)} %param.6) | copy-start | bytes 1769476
  7.2 138.6 %reduce-scatter.2.cloned.1.call-start = ((), (), s32[]{:S(2)}) async-start(), calls=%async_computation.4 | async-start | bytes 3342336 | tf_op jit(solution)/shard_map/reduce_scatter | solution.py:43
  42.0 11.5 %collective-permute-start = (bf16[16,2,32,384]{3,2,0,1:T(8,128)(2,1)S(1)}, bf16[16,2,32,384]{3,2,0,1:T(8,128)(2,1)S(1)}, u32[]{:S(2)}, u32[]{:S(2)}) collective-permute-start(bf16[16,2,32,384]{3,2,0,1:T(8,128)(2,1)S(1)} %copy.9), channel_id=1, source_target_pairs={{0,1},{1,0},{2,3},{3,2},{4,5},{5,4},{6,7},{7,6},{8,9},{9,8},{10,11... | collective-permute-start | bytes 2359304 | tf_op jit(solution)/shard_map/ppermute | solution.py:37
  56.4 1.1 copy-start.2
  56.6 1.9 copy-start.1
  148.9 24.3 %all-to-all-start.1 = ((bf16[16,64,768]{2,1,0:T(8,128)(2,1)}), bf16[16,64,768]{2,1,0:T(8,128)(2,1)S(1)}, u32[]{:S(2)}, u32[]{:S(2)}) async-start(bf16[16,64,768]{2,1,0:T(8,128)(2,1)} %broadcast_in_dim.2), calls=%async_computation.2 | async-start | bytes 3145728 | tf_op jit(solution)/shard_map/all_to_all | solution.py:50
  153.3 66.6 %all-gather.3.cloned.1.call-start = ((), (), s32[]{:S(2)}) async-start(), calls=%async_computation.5 | async-start | bytes 1671168 | tf_op jit(solution)/shard_map/all_gather | solution.py:48
  174.3 8.6 %collective-permute-start.1 = (f32[16,32,384]{2,1,0:T(8,128)S(1)}, f32[16,32,384]{2,1,0:T(8,128)S(1)}, u32[]{:S(2)}, u32[]{:S(2)}) collective-permute-start(f32[16,32,384]{2,1,0:T(8,128)S(1)} %bitcast.52), channel_id=1, source_target_pairs={{0,1},{1,0},{2,3},{3,2},{4,5},{5,4},{6,7},{7,6},{8,9},{9,8},{10,11... | collective-permute-start | bytes 2359304 | tf_op jit(solution)/shard_map/ppermute | solution.py:52
  183.7 39.9 %all-to-all-start.2 = ((bf16[16,32,384]{2,1,0:T(8,128)(2,1)}), bf16[16,32,384]{2,1,0:T(8,128)(2,1)S(1)}, u32[]{:S(2)}, u32[]{:S(2)}) async-start(bf16[16,32,384]{2,1,0:T(8,128)(2,1)} %add_convert_fusion), calls=%async_computation.3 | async-start | bytes 786432 | tf_op jit(solution)/shard_map/all_to_all | solution.py:53
Sparse Core Ops, SparseCore 0:
  56.5 89.2 reduce-scatter.1
  157.8 62.1 all-gather.2

commit v5 on v4

v5 whole, which is shorter than its diff:
```python
import jax
import jax.numpy as jnp
from jax import lax
from jax.sharding import Mesh
from jax.sharding import PartitionSpec as P

inv_sqrt_two = 0.7071067811865476
inv_sqrt_two_pi = 0.3989422804014327
ROW = ("y", "x")
COL = ("z", "core")
SWAP = [(0, 1), (1, 0)]


def normal_cdf(v):
    return 0.5 * (1.0 + lax.erf(v * inv_sqrt_two))


def normal_pdf(v):
    return jnp.exp(-0.5 * v * v) * inv_sqrt_two_pi


def dot(a, b, ca, cb):
    return lax.dot_general(a, b, (((ca,), (cb,)), ((), ())), preferred_element_type=jnp.float32)


def add_blocks(value):
    total = value[0].astype(jnp.float32)
    for i in range(1, value.shape[0]):
        total = total + value[i].astype(jnp.float32)
    return total


def gather_col(value):
    own = lax.all_gather(value, "z", axis=0, tiled=True)
    return jnp.concatenate([own, lax.ppermute(own, "core", SWAP)])


def sum_row(part):
    blocks = part.astype(jnp.bfloat16).reshape(16, -1, part.shape[-1])
    return add_blocks(lax.all_to_all(blocks, ROW, 0, 0, tiled=True))


def body(inputs, cotangent, weight_in, weight_out):
    rows, depth = inputs.shape
    hidden = weight_in.shape[1]
    x = gather_col(inputs)
    pre_part = dot(x, weight_in, 1, 0).astype(jnp.bfloat16)
    pre_part, cotangent = lax.optimization_barrier((pre_part, cotangent))
    preact = sum_row(pre_part)
    g = gather_col(cotangent)
    act_grad = sum_row(dot(g, weight_out, 1, 1))

    activated = (preact * normal_cdf(preact)).astype(jnp.bfloat16)
    act = lax.all_gather(activated, ROW, axis=0, tiled=True)
    pre_grad = (act_grad * (normal_cdf(preact) + preact * normal_pdf(preact))).astype(jnp.bfloat16)
    copies = jnp.broadcast_to(pre_grad[None], (16,) + pre_grad.shape)
    pg = lax.all_to_all(copies, ROW, 0, 0, tiled=True).reshape(-1, hidden)
    gi = dot(pg, weight_in, 1, 1).reshape(2, 16, rows, depth)
    chip = gi[0] + lax.ppermute(gi[1], "core", SWAP)
    pieces = lax.all_to_all(chip.astype(jnp.bfloat16), "z", 0, 0, tiled=True)
    grad_weight_in = dot(x, pg, 0, 0)
    grad_weight_out = dot(act, g, 0, 0)
    grad_inputs = add_blocks(pieces).astype(jnp.bfloat16)
    return (grad_inputs, grad_weight_in, grad_weight_out)


def solution(mesh):
    split = Mesh(mesh.devices.reshape(4, 4, 16, 2), ROW + COL)
    tok, w_in, w_out = P(COL, ROW), P(ROW, COL), P(COL, ROW)
    return jax.shard_map(
        body,
        mesh=split,
        in_specs=(tok, tok, w_in, w_out),
        out_specs=(tok, w_in, w_out),
        check_vma=False,
    )
```

time: 232 us -> 205 us (0.88)
  waiting for transfers between devices: 102 us -> 69.3 us
  starting transfers between devices: 32.8 us -> 48.9 us
  blocking collectives: 65.6 us -> 54.5 us
    reduce_scatter x1 -> x0, waiting for transfers between devices: 55.6 us -> none  [body(): preact = lax.psum_scatter(pre_part, ROW, scatter_dimension=0, tiled=True)]
    all_to_all x1 -> x0, blocking collectives: 31.7 us -> none  [body(): act_grad = add_blocks(lax.all_to_all(grad_part, ROW, 0, 0, tiled=True))]
    all_to_all x0 -> x2, waiting for transfers between devices: none -> 23.1 us  [sum_row(): return add_blocks(lax.all_to_all(blocks, ROW, 0, 0, tiled=True))]
    all_gather x1 -> x2, blocking collectives: 33.9 us -> 54.5 us  [gather_col(): own = lax.all_gather(value, 'z', axis=0, tiled=True)]
    all_to_all x0 -> x2, starting transfers between devices: none -> 14 us  [sum_row(): return add_blocks(lax.all_to_all(blocks, ROW, 0, 0, tiled=True))]
    ppermute x1 -> x2, starting transfers between devices: 9.64 us -> 17.6 us  [gather_col(): return jnp.concatenate([own, lax.ppermute(own, 'core', SWAP)])]
    all_to_all x1, starting transfers between devices: 12 us -> 7.44 us  [body(): pieces = lax.all_to_all(chip.astype(jnp.bfloat16), 'z', 0, 0, tiled=True)]
  transfers between devices with their start and end apart: 6 -> 8, of which waited for: 5 -> 6; matrix products, arithmetic and copies ran while one was open for 4% -> 5% of each run, Pallas kernels for 0% -> 0%
where the time goes in v5:
time: 205 us; the launch traced here: 204 us
  waiting for transfers between devices  69.3 us (34%)
  blocking collectives  54.5 us (27%)
  starting transfers between devices  48.9 us (24%)
  between operations  14.2 us (7%)
  matrix products  10.7 us (5%)
  other arithmetic  4.15 us (2%)
  local copies, waits for them, and re-layouts  2.52 us (1%)
    all_gather x2, blocking collectives, gather_col(): own = lax.all_gather(value, 'z', axis=0, tiled=True)  54.5 us
    all_to_all x2, waiting for transfers between devices, sum_row(): return add_blocks(lax.all_to_all(blocks, ROW, 0, 0, tiled=True))  23.1 us
    all_to_all x1, waiting for transfers between devices, body(): pg = lax.all_to_all(copies, ROW, 0, 0, tiled=True).reshape(-1, hidden)  20.6 us
    all_gather x1, waiting for transfers between devices, body(): act = lax.all_gather(activated, ROW, axis=0, tiled=True)  20.4 us
    ppermute x2, starting transfers between devices, gather_col(): return jnp.concatenate([own, lax.ppermute(own, 'core', SWAP)])  17.6 us
    all_to_all x2, starting transfers between devices, sum_row(): return add_blocks(lax.all_to_all(blocks, ROW, 0, 0, tiled=True))  14 us
    dot_general x5, matrix products, dot(): lax.dot_general(a, b, (((ca,), (cb,)), ((), ())), preferred_element_type=...  10.7 us
    all_to_all x1, starting transfers between devices, body(): pieces = lax.all_to_all(chip.astype(jnp.bfloat16), 'z', 0, 0, tiled=True)  7.44 us
  transfers between devices with their start and end apart: 8, of which 6 were waited for; matrix products, arithmetic and copies ran while one was open for 5% of the time, Pallas kernels for 0%

profile of v5, /device:TPU:1, one launch (start us, length us, event | category | flops | bytes accessed | tf_op | source)
XLA Modules:
  0.0 204.3 jit_solution(643306380360944810)
XLA Ops:
  7.2 31.5 %all_gather.9 = bf16[512,384]{1,0:T(8,128)(2,1)S(1)} all-gather(bf16[32,384]{1,0:T(8,128)(2,1)} %param.4), channel_id=1, replica_groups=mesh['y'=4,'x'=4,'z'=16,'core'=2] {'z'}, dimensions={0}, use_global_device_ids=true | all-gather | bytes 417792 | tf_op jit(solution)/shard_map/all_gather | solution.py:34
  38.6 10.0 %collective-permute-start = (bf16[512,384]{1,0:T(8,128)(2,1)S(1)}, bf16[512,384]{1,0:T(8,128)(2,1)S(1)}, u32[]{:S(2)}, u32[]{:S(2)}) collective-permute-start(bf16[512,384]{1,0:T(8,128)(2,1)S(1)} %all_gather.9), channel_id=1, source_target_pairs={{0,1},{1,0},{2,3},{3,2},{4,5},{5,4},{6,7},{7,6},{8,9},{9,8},{10,11... | collective-permute-start | bytes 1179656 | tf_op jit(solution)/shard_map/ppermute | solution.py:35
  48.7 1.3 collective-permute-done
  50.0 2.2 %convolution_convert_fusion.1 = bf16[1024,768]{1,0:T(8,128)(2,1)} fusion(bf16[1024,384]{1,0:T(8,128)(2,1)S(1)} %constant_dynamic-update-slice_fusion, bf16[384,768]{1,0:T(8,128)(2,1)S(1)} %copy-done), kind=kOutput, calls=%fused_computation.1 | convolution fusion | flops 604766208 | bytes 2949120 | tf_op jit(solution)/shard_map/dot_general | solution.py:23
  52.2 6.9 %all-to-all-start.1 = ((bf16[16,64,768]{2,1,0:T(8,128)(2,1)}), bf16[16,64,768]{2,1,0:T(8,128)(2,1)S(1)}, u32[]{:S(2)}, u32[]{:S(2)}) async-start(bf16[16,64,768]{2,1,0:T(8,128)(2,1)} %bitcast.37), calls=%async_computation.1 | async-start | bytes 3145728 | tf_op jit(solution)/shard_map/all_to_all | solution.py:40
  59.1 23.1 %all_gather.10 = bf16[512,384]{1,0:T(8,128)(2,1)S(1)} all-gather(bf16[32,384]{1,0:T(8,128)(2,1)S(1)} %copy-done.2), channel_id=1, replica_groups=mesh['y'=4,'x'=4,'z'=16,'core'=2] {'z'}, dimensions={0}, use_global_device_ids=true | all-gather | bytes 417792 | tf_op jit(solution)/shard_map/all_gather | solution.py:34
  82.2 7.7 %collective-permute-start.1 = (bf16[512,384]{1,0:T(8,128)(2,1)S(1)}, bf16[512,384]{1,0:T(8,128)(2,1)S(1)}, u32[]{:S(2)}, u32[]{:S(2)}) collective-permute-start(bf16[512,384]{1,0:T(8,128)(2,1)S(1)} %all_gather.10), channel_id=1, source_target_pairs={{0,1},{1,0},{2,3},{3,2},{4,5},{5,4},{6,7},{7,6},{8,9},{9,8},{10,11... | collective-permute-start | bytes 1179656 | tf_op jit(solution)/shard_map/ppermute | solution.py:35
  89.9 1.3 collective-permute-done.1
  91.2 0.9 copy-done.1
  92.1 2.1 %convolution_convert_fusion = bf16[1024,768]{1,0:T(8,128)(2,1)} fusion(bf16[1024,384]{1,0:T(8,128)(2,1)S(1)} %constant_dynamic-update-slice_fusion.2, bf16[768,384]{1,0:T(8,128)(2,1)S(1)} %copy-done.3), kind=kOutput, calls=%fused_computation | convolution fusion | flops 604766208 | bytes 2949120 | tf_op jit(solution)/shard_map/dot_general | solution.py:23
  94.3 7.1 %all-to-all-start = ((bf16[16,64,768]{2,1,0:T(8,128)(2,1)}), bf16[16,64,768]{2,1,0:T(8,128)(2,1)}, u32[]{:S(2)}, u32[]{:S(2)}) async-start(bf16[16,64,768]{2,1,0:T(8,128)(2,1)} %bitcast.38), calls=%async_computation | async-start | bytes 3145728 | tf_op jit(solution)/shard_map/all_to_all | solution.py:40
  101.4 0.9 multiply_convert_fusion
  102.3 23.1 %all-to-all-done = bf16[16,64,768]{2,1,0:T(8,128)(2,1)} async-done(((bf16[16,64,768]{2,1,0:T(8,128)(2,1)}), bf16[16,64,768]{2,1,0:T(8,128)(2,1)}, u32[]{:S(2)}, u32[]{:S(2)}) %all-to-all-start) | async-done | bytes 1572896 | tf_op jit(solution)/shard_map/all_to_all | solution.py:40
  125.4 1.8 fusion.7
  127.1 1.3 broadcast_in_dim.9
  128.4 4.1 %all-to-all-start.2 = ((bf16[16,64,768]{2,1,0:T(8,128)(2,1)}), bf16[16,64,768]{2,1,0:T(8,128)(2,1)S(1)}, u32[]{:S(2)}, u32[]{:S(2)}) async-start(bf16[16,64,768]{2,1,0:T(8,128)(2,1)} %broadcast_in_dim.9), calls=%async_computation.2 | async-start | bytes 3145728 | tf_op jit(solution)/shard_map/all_to_all | solution.py:57
  133.3 20.6 %all-to-all-done.2 = bf16[16,64,768]{2,1,0:T(8,128)(2,1)S(1)} async-done(((bf16[16,64,768]{2,1,0:T(8,128)(2,1)}), bf16[16,64,768]{2,1,0:T(8,128)(2,1)S(1)}, u32[]{:S(2)}, u32[]{:S(2)}) %all-to-all-start.2) | async-done | bytes 1572896 | tf_op jit(solution)/shard_map/all_to_all | solution.py:57
  153.9 1.0 fusion.10
  155.0 5.7 %collective-permute-start.2 = (f32[16,32,384]{2,1,0:T(8,128)S(1)}, f32[16,32,384]{2,1,0:T(8,128)S(1)}, u32[]{:S(2)}, u32[]{:S(2)}) collective-permute-start(f32[16,32,384]{2,1,0:T(8,128)S(1)} %bitcast.39), channel_id=1, source_target_pairs={{0,1},{1,0},{2,3},{3,2},{4,5},{5,4},{6,7},{7,6},{8,9},{9,8},{10,11... | collective-permute-start | bytes 2359304 | tf_op jit(solution)/shard_map/ppermute | solution.py:59
  160.7 1.9 collective-permute-done.2
  163.4 7.4 %all-to-all-start.3 = ((bf16[16,32,384]{2,1,0:T(8,128)(2,1)}), bf16[16,32,384]{2,1,0:T(8,128)(2,1)S(1)}, u32[]{:S(2)}, u32[]{:S(2)}) async-start(bf16[16,32,384]{2,1,0:T(8,128)(2,1)} %add_convert_fusion), calls=%async_computation.3 | async-start | bytes 786432 | tf_op jit(solution)/shard_map/all_to_all | solution.py:60
  170.9 1.8 fusion.11
  172.7 20.4 %all-gather.2.cloned.1.call-done = bf16[1024,768]{1,0:T(8,128)(2,1)} async-done(((bf16[64,768]{1,0:T(8,128)(2,1)}), bf16[1024,768]{1,0:T(8,128)(2,1)}) %all-gather.2.cloned.1.call-update) | async-done | bytes 1572880 | tf_op jit(solution)/shard_map/all_gather | solution.py:54
  193.1 3.6 %fusion.12 = f32[768,384]{1,0:T(8,128)} fusion(bf16[1024,768]{1,0:T(8,128)(2,1)} %all-gather.2.cloned.1.call-done, bf16[1024,384]{1,0:T(8,128)(2,1)} %copy-done.1), kind=kOutput, calls=%fused_computation.26 | convolution fusion | flops 603979776 | bytes 3538944 | tf_op jit(solution)/shard_map/dot_general | solution.py:23
  (18 shorter events, 2.6 us)
Async XLA Ops:
  7.2 42.9 %copy-start = (bf16[384,768]{1,0:T(8,128)(2,1)S(1)}, bf16[384,768]{1,0:T(8,128)(2,1)}, u32[]{:S(2)}) copy-start(bf16[384,768]{1,0:T(8,128)(2,1)} %param.6) | copy-start | bytes 1769476
  38.6 11.3 %collective-permute-start = (bf16[512,384]{1,0:T(8,128)(2,1)S(1)}, bf16[512,384]{1,0:T(8,128)(2,1)S(1)}, u32[]{:S(2)}, u32[]{:S(2)}) collective-permute-start(bf16[512,384]{1,0:T(8,128)(2,1)S(1)} %all_gather.9), channel_id=1, source_target_pairs={{0,1},{1,0},{2,3},{3,2},{4,5},{5,4},{6,7},{7,6},{8,9},{9,8},{10,11... | collective-permute-start | bytes 1179656 | tf_op jit(solution)/shard_map/ppermute | solution.py:35
  52.2 6.9 %copy-start.2 = (bf16[32,384]{1,0:T(8,128)(2,1)S(1)}, bf16[32,384]{1,0:T(8,128)(2,1)}, u32[]{:S(2)}) copy-start(bf16[32,384]{1,0:T(8,128)(2,1)} %param.5) | copy-start | bytes 73732
  52.2 42.1 %all-to-all-start.1 = ((bf16[16,64,768]{2,1,0:T(8,128)(2,1)}), bf16[16,64,768]{2,1,0:T(8,128)(2,1)S(1)}, u32[]{:S(2)}, u32[]{:S(2)}) async-start(bf16[16,64,768]{2,1,0:T(8,128)(2,1)} %bitcast.37), calls=%async_computation.1 | async-start | bytes 3145728 | tf_op jit(solution)/shard_map/all_to_all | solution.py:40
  59.1 33.0 %copy-start.3 = (bf16[768,384]{1,0:T(8,128)(2,1)S(1)}, bf16[768,384]{1,0:T(8,128)(2,1)}, u32[]{:S(2)}) copy-start(bf16[768,384]{1,0:T(8,128)(2,1)} %param.7) | copy-start | bytes 1769476
  82.2 9.0 %collective-permute-start.1 = (bf16[512,384]{1,0:T(8,128)(2,1)S(1)}, bf16[512,384]{1,0:T(8,128)(2,1)S(1)}, u32[]{:S(2)}, u32[]{:S(2)}) collective-permute-start(bf16[512,384]{1,0:T(8,128)(2,1)S(1)} %all_gather.10), channel_id=1, source_target_pairs={{0,1},{1,0},{2,3},{3,2},{4,5},{5,4},{6,7},{7,6},{8,9},{9,8},{10,11... | collective-permute-start | bytes 1179656 | tf_op jit(solution)/shard_map/ppermute | solution.py:35
  91.2 0.9 copy-start.1
  94.3 31.1 %all-to-all-start = ((bf16[16,64,768]{2,1,0:T(8,128)(2,1)}), bf16[16,64,768]{2,1,0:T(8,128)(2,1)}, u32[]{:S(2)}, u32[]{:S(2)}) async-start(bf16[16,64,768]{2,1,0:T(8,128)(2,1)} %bitcast.38), calls=%async_computation | async-start | bytes 3145728 | tf_op jit(solution)/shard_map/all_to_all | solution.py:40
  128.4 25.5 %all-to-all-start.2 = ((bf16[16,64,768]{2,1,0:T(8,128)(2,1)}), bf16[16,64,768]{2,1,0:T(8,128)(2,1)S(1)}, u32[]{:S(2)}, u32[]{:S(2)}) async-start(bf16[16,64,768]{2,1,0:T(8,128)(2,1)} %broadcast_in_dim.9), calls=%async_computation.2 | async-start | bytes 3145728 | tf_op jit(solution)/shard_map/all_to_all | solution.py:57
  132.5 60.6 %all-gather.2.cloned.1.call-start = ((), (), s32[]{:S(2)}) async-start(), calls=%async_computation.4 | async-start | bytes 1671168 | tf_op jit(solution)/shard_map/all_gather | solution.py:54
  155.0 7.6 %collective-permute-start.2 = (f32[16,32,384]{2,1,0:T(8,128)S(1)}, f32[16,32,384]{2,1,0:T(8,128)S(1)}, u32[]{:S(2)}, u32[]{:S(2)}) collective-permute-start(f32[16,32,384]{2,1,0:T(8,128)S(1)} %bitcast.39), channel_id=1, source_target_pairs={{0,1},{1,0},{2,3},{3,2},{4,5},{5,4},{6,7},{7,6},{8,9},{9,8},{10,11... | collective-permute-start | bytes 2359304 | tf_op jit(solution)/shard_map/ppermute | solution.py:59
  163.4 33.3 %all-to-all-start.3 = ((bf16[16,32,384]{2,1,0:T(8,128)(2,1)}), bf16[16,32,384]{2,1,0:T(8,128)(2,1)S(1)}, u32[]{:S(2)}, u32[]{:S(2)}) async-start(bf16[16,32,384]{2,1,0:T(8,128)(2,1)} %add_convert_fusion), calls=%async_computation.3 | async-start | bytes 786432 | tf_op jit(solution)/shard_map/all_to_all | solution.py:60
Sparse Core Ops, SparseCore 0:
  136.9 56.1 all-gather.1

commit v6 on v5

--- a/solution.py
+++ b/solution.py
@@ -8,6 +8,7 @@
 inv_sqrt_two_pi = 0.3989422804014327
 ROW = ("y", "x")
 COL = ("z", "core")
+PLANE = ("y", "x", "core")
 SWAP = [(0, 1), (1, 0)]
 
 
@@ -30,25 +31,40 @@
     return total
 
 
-def gather_col(value):
-    own = lax.all_gather(value, "z", axis=0, tiled=True)
-    return jnp.concatenate([own, lax.ppermute(own, "core", SWAP)])
+def rings(axis):
+    groups = []
+    for core in range(2):
+        for i in range(4):
+            if core == axis:
+                groups.append([(i * 4 + j) * 2 + core for j in range(4)])
+            else:
+                groups.append([(j * 4 + i) * 2 + core for j in range(4)])
+    return groups
 
 
-def sum_row(part):
-    blocks = part.astype(jnp.bfloat16).reshape(16, -1, part.shape[-1])
-    return add_blocks(lax.all_to_all(blocks, ROW, 0, 0, tiled=True))
+def add_ring(blocks, axis):
+    blocks = blocks.astype(jnp.bfloat16)
+    return add_blocks(lax.all_to_all(blocks, PLANE, 0, 0, tiled=True, axis_index_groups=rings(axis)))
 
 
 def body(inputs, cotangent, weight_in, weight_out):
     rows, depth = inputs.shape
     hidden = weight_in.shape[1]
-    x = gather_col(inputs)
-    pre_part = dot(x, weight_in, 1, 0).astype(jnp.bfloat16)
-    pre_part, cotangent = lax.optimization_barrier((pre_part, cotangent))
-    preact = sum_row(pre_part)
-    g = gather_col(cotangent)
-    act_grad = sum_row(dot(g, weight_out, 1, 1))
+    own = lax.all_gather(jnp.stack([inputs, cotangent]), "z", axis=0)
+    other = lax.ppermute(own, "core", SWAP)
+    x = jnp.concatenate([own[:, 0], other[:, 0]]).reshape(-1, depth)
+    g = jnp.concatenate([own[:, 1], other[:, 1]]).reshape(-1, depth)
+    share = x.shape[0] // 16
+
+    def by_ring(value):
+        sheet = value.reshape(4, 4, share, depth)
+        turned = jnp.where(lax.axis_index("core") == 0, sheet.swapaxes(0, 1), sheet)
+        return turned.reshape(-1, depth)
+
+    pre_part = dot(by_ring(x), weight_in, 1, 0).astype(jnp.bfloat16).reshape(4, 4, share, hidden)
+    grad_part = dot(by_ring(g), weight_out, 1, 1).astype(jnp.bfloat16).reshape(4, 4, share, hidden)
+    sums = add_ring(add_ring(jnp.stack([pre_part, grad_part], axis=2), 0), 1)
+    preact, act_grad = sums[0], sums[1]
 
     activated = (preact * normal_cdf(preact)).astype(jnp.bfloat16)
     act = lax.all_gather(activated, ROW, axis=0, tiled=True)

time: 205 us -> 173 us (0.84)
  waiting for transfers between devices: 69.3 us -> 44.9 us
  starting transfers between devices: 48.9 us -> 27.1 us
  blocking collectives: 54.5 us -> 71 us
  matrix products: 10.7 us -> 8.42 us
    all_to_all x0 -> x2, blocking collectives: none -> 37.1 us  [add_ring(): lax.all_to_all(blocks, PLANE, 0, 0, tiled=True, axis_index_groups=rings(a...]
    all_to_all x2 -> x0, waiting for transfers between devices: 23.1 us -> none  [sum_row(): return add_blocks(lax.all_to_all(blocks, ROW, 0, 0, tiled=True))]
    all_gather x2 -> x1, blocking collectives: 54.5 us -> 33.9 us  [body(): own = lax.all_gather(jnp.stack([inputs, cotangent]), 'z', axis=0)]
    all_to_all x2 -> x0, starting transfers between devices: 14 us -> none  [sum_row(): return add_blocks(lax.all_to_all(blocks, ROW, 0, 0, tiled=True))]
    ppermute x2 -> x1, starting transfers between devices: 17.6 us -> 9.64 us  [body(): other = lax.ppermute(own, 'core', SWAP)]
    dot_general x5, matrix products: 10.7 us -> 8.42 us  [dot(): lax.dot_general(a, b, (((ca,), (cb,)), ((), ())), preferred_element_type=...]
    all_gather x1, waiting for transfers between devices: 20.4 us -> 22.5 us  [body(): act = lax.all_gather(activated, ROW, axis=0, tiled=True)]
  transfers between devices with their start and end apart: 8 -> 5, of which waited for: 6 -> 4; matrix products, arithmetic and copies ran while one was open for 5% -> 5% of each run, Pallas kernels for 0% -> 0%
where the time goes in v6:
time: 173 us
  blocking collectives  71 us (41%)
  waiting for transfers between devices  44.9 us (26%)
  starting transfers between devices  27.1 us (16%)
  between operations  14.2 us (8%)
  matrix products  8.42 us (5%)
  other arithmetic  4.24 us (2%)
  local copies, waits for them, and re-layouts  2.87 us (2%)
    all_to_all x2, blocking collectives, add_ring(): lax.all_to_all(blocks, PLANE, 0, 0, tiled=True, axis_index_groups=rings(a...  37.1 us
    all_gather x1, blocking collectives, body(): own = lax.all_gather(jnp.stack([inputs, cotangent]), 'z', axis=0)  33.9 us
    all_gather x1, waiting for transfers between devices, body(): act = lax.all_gather(activated, ROW, axis=0, tiled=True)  22.5 us
    all_to_all x1, waiting for transfers between devices, body(): pg = lax.all_to_all(copies, ROW, 0, 0, tiled=True).reshape(-1, hidden)  18.7 us
    ppermute x1, starting transfers between devices, body(): other = lax.ppermute(own, 'core', SWAP)  9.64 us
    dot_general x5, matrix products, dot(): lax.dot_general(a, b, (((ca,), (cb,)), ((), ())), preferred_element_type=...  8.42 us
    ppermute x1, starting transfers between devices, body(): chip = gi[0] + lax.ppermute(gi[1], 'core', SWAP)  7.3 us
    all_to_all x1, starting transfers between devices, body(): pieces = lax.all_to_all(chip.astype(jnp.bfloat16), 'z', 0, 0, tiled=True)  6.37 us
  transfers between devices with their start and end apart: 5, of which 4 were waited for; matrix products, arithmetic and copies ran while one was open for 5% of the time, Pallas kernels for 0%

profile of v6, /device:TPU:1, one launch (start us, length us, event | category | flops | bytes accessed | tf_op | source)
XLA Modules:
  0.0 172.8 jit_solution(10461462603780096722)
XLA Ops:
  7.2 0.8 pad_maximum_fusion.3
  8.0 33.9 %all-gather = bf16[32,32,384]{2,1,0:T(8,128)(2,1)S(1)} all-gather(bf16[2,32,384]{2,1,0:T(8,128)(2,1)S(1)} %pad_maximum_fusion.3), channel_id=2, replica_groups=mesh['y'=4,'x'=4,'z'=16,'core'=2] {'z'}, dimensions={0}, use_global_device_ids=true | all-gather | bytes 835584 | tf_op jit(solution)/shard_map/all_gather | solution.py:53
  42.0 9.6 %collective-permute-start = (bf16[16,2,32,384]{3,2,0,1:T(8,128)(2,1)S(1)}, bf16[16,2,32,384]{3,2,0,1:T(8,128)(2,1)S(1)}, u32[]{:S(2)}, u32[]{:S(2)}) collective-permute-start(bf16[16,2,32,384]{3,2,0,1:T(8,128)(2,1)S(1)} %copy.12), channel_id=1, source_target_pairs={{0,1},{1,0},{2,3},{3,2},{4,5},{5,4},{6,7},{7,6},{8,9},{9,8},{10,11... | collective-permute-start | bytes 2359304 | tf_op jit(solution)/shard_map/ppermute | solution.py:54
  51.7 1.8 %collective-permute-done = bf16[16,2,32,384]{3,2,0,1:T(8,128)(2,1)S(1)} collective-permute-done((bf16[16,2,32,384]{3,2,0,1:T(8,128)(2,1)S(1)}, bf16[16,2,32,384]{3,2,0,1:T(8,128)(2,1)S(1)}, u32[]{:S(2)}, u32[]{:S(2)}) %collective-permute-start) | collective-permute-done | bytes 786464 | tf_op jit(solution)/shard_map/ppermute | solution.py:54
  54.0 0.7 copy-done.1
  54.7 0.5 copy-done.2
  55.2 1.0 convolution_convert_fusion
  56.2 1.0 convolution_convert_fusion.1
  57.5 25.3 %all_to_all.20 = bf16[4,4,2,64,768]{4,3,1,2,0:T(8,128)(2,1)S(1)} all-to-all(bf16[4,4,2,64,768]{4,3,1,2,0:T(8,128)(2,1)S(1)} %pad_maximum_fusion), channel_id=1, replica_groups={{0,32,64,96},{128,160,192,224},{256,288,320,352},{384,416,448,480},{1,1..., dimensions={0} | all-to-all | bytes 6291456 | tf_op jit(solution)/shard_map/all_to_all | solution.py:47
  82.7 0.4 fusion
  83.2 11.9 %all_to_all.21 = bf16[4,2,64,768]{3,2,1,0:T(8,128)(2,1)S(1)} all-to-all(bf16[4,2,64,768]{3,2,1,0:T(8,128)(2,1)S(1)} %copy.18), channel_id=1, replica_groups={{0,128,256,384},{32,160,288,416},{64,192,320,448},{96,224,352,480},{1,3..., dimensions={0} | all-to-all | bytes 1572864 | tf_op jit(solution)/shard_map/all_to_all | solution.py:47
  95.3 1.3 broadcast_in_dim.9
  96.6 3.7 %all-to-all-start.2 = ((bf16[16,64,768]{2,1,0:T(8,128)(2,1)}), bf16[16,64,768]{2,1,0:T(8,128)(2,1)S(1)}, u32[]{:S(2)}, u32[]{:S(2)}) async-start(bf16[16,64,768]{2,1,0:T(8,128)(2,1)} %broadcast_in_dim.9), calls=%async_computation.2 | async-start | bytes 3145728 | tf_op jit(solution)/shard_map/all_to_all | solution.py:73
  100.3 0.7 fusion.13
  101.0 18.7 %all-to-all-done.2 = bf16[16,64,768]{2,1,0:T(8,128)(2,1)S(1)} async-done(((bf16[16,64,768]{2,1,0:T(8,128)(2,1)}), bf16[16,64,768]{2,1,0:T(8,128)(2,1)S(1)}, u32[]{:S(2)}, u32[]{:S(2)}) %all-to-all-start.2) | async-done | bytes 1572896 | tf_op jit(solution)/shard_map/all_to_all | solution.py:73
  119.7 1.0 fusion.17
  120.8 7.3 %collective-permute-start.1 = (f32[16,32,384]{2,1,0:T(8,128)S(1)}, f32[16,32,384]{2,1,0:T(8,128)S(1)}, u32[]{:S(2)}, u32[]{:S(2)}) collective-permute-start(f32[16,32,384]{2,1,0:T(8,128)S(1)} %bitcast.98), channel_id=1, source_target_pairs={{0,1},{1,0},{2,3},{3,2},{4,5},{5,4},{6,7},{7,6},{8,9},{9,8},{10,11... | collective-permute-start | bytes 2359304 | tf_op jit(solution)/shard_map/ppermute | solution.py:75
  128.1 1.9 %collective-permute-done.1 = f32[16,32,384]{2,1,0:T(8,128)S(1)} collective-permute-done((f32[16,32,384]{2,1,0:T(8,128)S(1)}, f32[16,32,384]{2,1,0:T(8,128)S(1)}, u32[]{:S(2)}, u32[]{:S(2)}) %collective-permute-start.1) | collective-permute-done | bytes 786464 | tf_op jit(solution)/shard_map/ppermute | solution.py:75
  130.0 0.8 add_convert_fusion.1
  130.9 6.4 %all-to-all-start.3 = ((bf16[16,32,384]{2,1,0:T(8,128)(2,1)}), bf16[16,32,384]{2,1,0:T(8,128)(2,1)S(1)}, u32[]{:S(2)}, u32[]{:S(2)}) async-start(bf16[16,32,384]{2,1,0:T(8,128)(2,1)} %add_convert_fusion.1), calls=%async_computation.3 | async-start | bytes 786432 | tf_op jit(solution)/shard_map/all_to_all | solution.py:76
  137.3 1.8 %fusion.18 = f32[384,768]{1,0:T(8,128)} fusion(bf16[1024,384]{1,0:T(8,128)(2,1)S(1)} %bitcast.87, bf16[1024,768]{1,0:T(8,128)(2,1)S(1)} %bitcast.84), kind=kOutput, calls=%fused_computation.40 | convolution fusion | flops 603979776 | bytes 3538944 | tf_op jit(solution)/shard_map/dot_general | solution.py:24
  139.1 22.5 %all-gather.3.cloned.1.call-done = bf16[1024,768]{1,0:T(8,128)(2,1)} async-done(((bf16[64,768]{1,0:T(8,128)(2,1)}), bf16[1024,768]{1,0:T(8,128)(2,1)}) %all-gather.3.cloned.1.call-update) | async-done | bytes 1572880 | tf_op jit(solution)/shard_map/all_gather | solution.py:70
  161.6 3.6 %fusion.19 = f32[768,384]{1,0:T(8,128)} fusion(bf16[1024,768]{1,0:T(8,128)(2,1)} %all-gather.3.cloned.1.call-done, bf16[1024,384]{1,0:T(8,128)(2,1)} %bitcast.92), kind=kOutput, calls=%fused_computation.41 | convolution fusion | flops 603979776 | bytes 3538944 | tf_op jit(solution)/shard_map/dot_general | solution.py:24
  165.2 0.7 fusion.15
  (19 shorter events, 1.3 us)
Async XLA Ops:
  7.2 49.0 %copy-start = (bf16[384,768]{1,0:T(8,128)(2,1)S(1)}, bf16[384,768]{1,0:T(8,128)(2,1)}, u32[]{:S(2)}) copy-start(bf16[384,768]{1,0:T(8,128)(2,1)} %param.6) | copy-start | bytes 1769476
  42.0 11.5 %collective-permute-start = (bf16[16,2,32,384]{3,2,0,1:T(8,128)(2,1)S(1)}, bf16[16,2,32,384]{3,2,0,1:T(8,128)(2,1)S(1)}, u32[]{:S(2)}, u32[]{:S(2)}) collective-permute-start(bf16[16,2,32,384]{3,2,0,1:T(8,128)(2,1)S(1)} %copy.12), channel_id=1, source_target_pairs={{0,1},{1,0},{2,3},{3,2},{4,5},{5,4},{6,7},{7,6},{8,9},{9,8},{10,11... | collective-permute-start | bytes 2359304 | tf_op jit(solution)/shard_map/ppermute | solution.py:54
  53.8 0.9 copy-start.1
  53.9 1.3 copy-start.2
  96.6 23.2 %all-to-all-start.2 = ((bf16[16,64,768]{2,1,0:T(8,128)(2,1)}), bf16[16,64,768]{2,1,0:T(8,128)(2,1)S(1)}, u32[]{:S(2)}, u32[]{:S(2)}) async-start(bf16[16,64,768]{2,1,0:T(8,128)(2,1)} %broadcast_in_dim.9), calls=%async_computation.2 | async-start | bytes 3145728 | tf_op jit(solution)/shard_map/all_to_all | solution.py:73
  100.3 61.3 %all-gather.3.cloned.1.call-start = ((), (), s32[]{:S(2)}) async-start(), calls=%async_computation.4 | async-start | bytes 1671168 | tf_op jit(solution)/shard_map/all_gather | solution.py:70
  120.8 9.2 %collective-permute-start.1 = (f32[16,32,384]{2,1,0:T(8,128)S(1)}, f32[16,32,384]{2,1,0:T(8,128)S(1)}, u32[]{:S(2)}, u32[]{:S(2)}) collective-permute-start(f32[16,32,384]{2,1,0:T(8,128)S(1)} %bitcast.98), channel_id=1, source_target_pairs={{0,1},{1,0},{2,3},{3,2},{4,5},{5,4},{6,7},{7,6},{8,9},{9,8},{10,11... | collective-permute-start | bytes 2359304 | tf_op jit(solution)/shard_map/ppermute | solution.py:75
  130.9 34.4 %all-to-all-start.3 = ((bf16[16,32,384]{2,1,0:T(8,128)(2,1)}), bf16[16,32,384]{2,1,0:T(8,128)(2,1)S(1)}, u32[]{:S(2)}, u32[]{:S(2)}) async-start(bf16[16,32,384]{2,1,0:T(8,128)(2,1)} %add_convert_fusion.1), calls=%async_computation.3 | async-start | bytes 786432 | tf_op jit(solution)/shard_map/all_to_all | solution.py:76
Sparse Core Ops, SparseCore 0:
  104.7 56.8 all-gather.2

commit v7 on v6

--- a/solution.py
+++ b/solution.py
@@ -42,9 +42,30 @@
     return groups
 
 
-def add_ring(blocks, axis):
-    blocks = blocks.astype(jnp.bfloat16)
-    return add_blocks(lax.all_to_all(blocks, PLANE, 0, 0, tiled=True, axis_index_groups=rings(axis)))
+def add_ring(blocks, own, pos, axis):
+    landed = lax.all_to_all(blocks, PLANE, 0, 0, tiled=True, axis_index_groups=rings(axis))
+    total = own
+    for i in range(4):
+        total = total + jnp.where(i == pos, 0.0, landed[i].astype(jnp.float32))
+    return total
+
+
+def hop(value, axis, step):
+    pairs = []
+    for ring in rings(axis):
+        pairs += [(ring[i], ring[(i + step) % 4]) for i in range(4)]
+    return lax.ppermute(value, PLANE, pairs)
+
+
+def gather_from(value, axis):
+    pieces = [value] + [hop(value, axis, 4 - step) for step in range(1, 4)]
+    return jnp.concatenate(pieces)
+
+
+def turn(value, axis, by):
+    return lax.dynamic_slice_in_dim(
+        jnp.concatenate([value, value], axis=axis), by, value.shape[axis], axis
+    )
 
 
 def body(inputs, cotangent, weight_in, weight_out):
@@ -56,26 +77,43 @@
     g = jnp.concatenate([own[:, 1], other[:, 1]]).reshape(-1, depth)
     share = x.shape[0] // 16
 
+    first = lax.axis_index("core") == 0
+    pos_y, pos_x = lax.axis_index("y"), lax.axis_index("x")
+    pos_a, pos_b = jnp.where(first, pos_x, pos_y), jnp.where(first, pos_y, pos_x)
+
     def by_ring(value):
         sheet = value.reshape(4, 4, share, depth)
-        turned = jnp.where(lax.axis_index("core") == 0, sheet.swapaxes(0, 1), sheet)
-        return turned.reshape(-1, depth)
+        return jnp.where(first, sheet.swapaxes(0, 1), sheet)
 
-    pre_part = dot(by_ring(x), weight_in, 1, 0).astype(jnp.bfloat16).reshape(4, 4, share, hidden)
-    grad_part = dot(by_ring(g), weight_out, 1, 1).astype(jnp.bfloat16).reshape(4, 4, share, hidden)
-    sums = add_ring(add_ring(jnp.stack([pre_part, grad_part], axis=2), 0), 1)
+    x_ring, g_ring = by_ring(x), by_ring(g)
+    flat = (-1, depth)
+    pre_part = dot(x_ring.reshape(flat), weight_in, 1, 0).astype(jnp.bfloat16)
+    grad_part = dot(g_ring.reshape(flat), weight_out, 1, 1).astype(jnp.bfloat16)
+    parts = [part.reshape(4, 4, share, hidden) for part in (pre_part, grad_part)]
+    own_x = lax.dynamic_index_in_dim(x_ring, pos_a, 0, keepdims=False).reshape(flat)
+    own_g = lax.dynamic_index_in_dim(g_ring, pos_a, 0, keepdims=False).reshape(flat)
+    own_parts = [dot(own_x, weight_in, 1, 0), dot(own_g, weight_out, 1, 1)]
+    own_parts = [part.reshape(4, share, hidden) for part in own_parts]
+    line = add_ring(jnp.stack(parts, axis=2), jnp.stack(own_parts, axis=1), pos_a, 0)
+    own_line = lax.dynamic_index_in_dim(line, pos_b, 0, keepdims=False)
+    sums = add_ring(line.astype(jnp.bfloat16), own_line, pos_b, 1)
     preact, act_grad = sums[0], sums[1]
 
     activated = (preact * normal_cdf(preact)).astype(jnp.bfloat16)
-    act = lax.all_gather(activated, ROW, axis=0, tiled=True)
+    act_line = gather_from(activated, 1)
     pre_grad = (act_grad * (normal_cdf(preact) + preact * normal_pdf(preact))).astype(jnp.bfloat16)
     copies = jnp.broadcast_to(pre_grad[None], (16,) + pre_grad.shape)
     pg = lax.all_to_all(copies, ROW, 0, 0, tiled=True).reshape(-1, hidden)
+    pg, act_line = lax.optimization_barrier((pg, act_line))
     gi = dot(pg, weight_in, 1, 1).reshape(2, 16, rows, depth)
-    chip = gi[0] + lax.ppermute(gi[1], "core", SWAP)
-    pieces = lax.all_to_all(chip.astype(jnp.bfloat16), "z", 0, 0, tiled=True)
+    chip = (gi[0] + lax.ppermute(gi[1], "core", SWAP)).astype(jnp.bfloat16)
+    chip, pg = lax.optimization_barrier((chip, pg))
+    pieces = lax.all_to_all(chip, "z", 0, 0, tiled=True)
     grad_weight_in = dot(x, pg, 0, 0)
-    grad_weight_out = dot(act, g, 0, 0)
+    grad_weight_in, act_line = lax.optimization_barrier((grad_weight_in, act_line))
+    act = gather_from(act_line, 0)
+    g_from = turn(turn(g_ring, 0, pos_a), 1, pos_b).reshape(flat)
+    grad_weight_out = dot(act, g_from, 0, 0)
     grad_inputs = add_blocks(pieces).astype(jnp.bfloat16)
     return (grad_inputs, grad_weight_in, grad_weight_out)
 

time: 173 us -> 164 us (0.948)
  blocking collectives: 71 us -> 33.9 us
  starting transfers between devices: 27.1 us -> 52 us
  between operations: 14.2 us -> 0.91 us
  other arithmetic: 4.24 us -> 12.2 us
  waiting for transfers between devices: 44.9 us -> 49.6 us
    all_to_all x2 -> x0, blocking collectives: 37.1 us -> none  [add_ring(): lax.all_to_all(blocks, PLANE, 0, 0, tiled=True, axis_index_groups=rings(a...]
    all_to_all x1 -> x3, waiting for transfers between devices: 0.01 us -> 27.9 us  [the longest x2 27.9 us: add_ring(): lax.all_to_all(blocks, PLANE, 0, 0, tiled=True, axis_index_groups=rings(a...]
    all_gather x1 -> x0, waiting for transfers between devices: 22.5 us -> none  [body(): act = lax.all_gather(activated, ROW, axis=0, tiled=True)]
    all_to_all x1, waiting for transfers between devices: 18.7 us -> 0.01 us  [body(): pg = lax.all_to_all(copies, ROW, 0, 0, tiled=True).reshape(-1, hidden)]
    ppermute x1 -> x7, waiting for transfers between devices: 1.89 us -> 19.9 us  [the longest x6 18 us: hop(): return lax.ppermute(value, PLANE, pairs)]
    ppermute x1 -> x7, starting transfers between devices: 7.3 us -> 23.9 us  [the longest x6 18.9 us: hop(): return lax.ppermute(value, PLANE, pairs)]
    all_to_all x1 -> x3, starting transfers between devices: 6.37 us -> 14.7 us  [the longest x2 8.37 us: add_ring(): lax.all_to_all(blocks, PLANE, 0, 0, tiled=True, axis_index_groups=rings(a...]
    convert_element_type x1 -> x2, other arithmetic: 0.84 us -> 4.48 us  [the longest x1 3.65 us: body(): sums = add_ring(line.astype(jnp.bfloat16), own_line, pos_b, 1)]
  transfers between devices with their start and end apart: 5 -> 12, of which waited for: 4 -> 7; matrix products, arithmetic and copies ran while one was open for 5% -> 6% of each run, Pallas kernels for 0% -> 0%
where the time goes in v7:
time: 164 us; the launch traced here: 163 us
  starting transfers between devices  52 us (32%)
  waiting for transfers between devices  49.6 us (30%)
  blocking collectives  33.9 us (21%)
  other arithmetic  12.2 us (7%)
  matrix products  9.49 us (6%)
  local copies, waits for them, and re-layouts  4.56 us (3%)
    all_gather x1, blocking collectives, body(): own = lax.all_gather(jnp.stack([inputs, cotangent]), 'z', axis=0)  33.9 us
    all_to_all x2, waiting for transfers between devices, add_ring(): lax.all_to_all(blocks, PLANE, 0, 0, tiled=True, axis_index_groups=rings(a...  27.9 us
    ppermute x6, starting transfers between devices, hop(): return lax.ppermute(value, PLANE, pairs)  18.9 us
    ppermute x6, waiting for transfers between devices, hop(): return lax.ppermute(value, PLANE, pairs)  18 us
    ppermute x1, starting transfers between devices, body(): other = lax.ppermute(own, 'core', SWAP)  9.64 us
    dot_general x7, matrix products, dot(): lax.dot_general(a, b, (((ca,), (cb,)), ((), ())), preferred_element_type=...  9.49 us
    all_to_all x2, starting transfers between devices, add_ring(): lax.all_to_all(blocks, PLANE, 0, 0, tiled=True, axis_index_groups=rings(a...  8.37 us
    all_to_all x1, starting transfers between devices, body(): pieces = lax.all_to_all(chip, 'z', 0, 0, tiled=True)  6.37 us
  transfers between devices with their start and end apart: 12, of which 7 were waited for; matrix products, arithmetic and copies ran while one was open for 6% of the time, Pallas kernels for 0%

profile of v7, /device:TPU:1, one launch (start us, length us, event | category | flops | bytes accessed | tf_op | source)
XLA Modules:
  0.0 162.7 jit_solution(1923629700245920956)
XLA Ops:
  1.5 33.9 %all-gather = bf16[32,32,384]{2,1,0:T(8,128)(2,1)S(1)} all-gather(bf16[2,32,384]{2,1,0:T(8,128)(2,1)S(1)} %pad_maximum_fusion.4), channel_id=2, replica_groups=mesh['y'=4,'x'=4,'z'=16,'core'=2] {'z'}, dimensions={0}, use_global_device_ids=true | all-gather | bytes 835584 | tf_op jit(solution)/shard_map/all_gather | solution.py:74
  35.5 9.6 %collective-permute-start = (bf16[16,2,32,384]{3,2,0,1:T(8,128)(2,1)S(1)}, bf16[16,2,32,384]{3,2,0,1:T(8,128)(2,1)S(1)}, u32[]{:S(2)}, u32[]{:S(2)}) collective-permute-start(bf16[16,2,32,384]{3,2,0,1:T(8,128)(2,1)S(1)} %copy.12), channel_id=1, source_target_pairs={{0,1},{1,0},{2,3},{3,2},{4,5},{5,4},{6,7},{7,6},{8,9},{9,8},{10,11... | collective-permute-start | bytes 2359304 | tf_op jit(solution)/shard_map/ppermute | solution.py:75
  45.2 1.8 %collective-permute-done = bf16[16,2,32,384]{3,2,0,1:T(8,128)(2,1)S(1)} collective-permute-done((bf16[16,2,32,384]{3,2,0,1:T(8,128)(2,1)S(1)}, bf16[16,2,32,384]{3,2,0,1:T(8,128)(2,1)S(1)}, u32[]{:S(2)}, u32[]{:S(2)}) %collective-permute-start) | collective-permute-done | bytes 786464 | tf_op jit(solution)/shard_map/ppermute | solution.py:75
  51.4 2.0 %pad_maximum_fusion = bf16[4,4,2,64,768]{4,3,1,2,0:T(8,128)(2,1)} fusion(bf16[4,4,1,64,768]{4,3,1,2,0:T(8,128)(2,1)S(1)} %bitcast.135, bf16[4,4,1,64,768]{4,3,1,2,0:T(8,128)(2,1)S(1)} %bitcast.136), kind=kLoop, calls=%fused_computation | loop fusion | flops 1572864 | bytes 6291456 | tf_op jit(solution)/shard_map/stack | solution.py:97
  53.4 4.6 %all-to-all-start = ((bf16[4,4,2,64,768]{4,3,1,2,0:T(8,128)(2,1)}), bf16[4,4,2,64,768]{4,3,1,2,0:T(8,128)(2,1)}, u32[]{:S(2)}, u32[]{:S(2)}) async-start(bf16[4,4,2,64,768]{4,3,1,2,0:T(8,128)(2,1)} %pad_maximum_fusion), calls=%async_computation | async-start | bytes 6291456 | tf_op jit(solution)/shard_map/all_to_all | solution.py:46
  59.8 19.6 %all-to-all-done = bf16[4,4,2,64,768]{4,3,1,2,0:T(8,128)(2,1)} async-done(((bf16[4,4,2,64,768]{4,3,1,2,0:T(8,128)(2,1)}), bf16[4,4,2,64,768]{4,3,1,2,0:T(8,128)(2,1)}, u32[]{:S(2)}, u32[]{:S(2)}) %all-to-all-start) | async-done | bytes 3145760 | tf_op jit(solution)/shard_map/all_to_all | solution.py:46
  79.4 3.6 %fusion.37 = (bf16[4,2,64,768]{3,2,0,1:T(8,128)(2,1)S(1)}, f32[4,2,64,768]{3,2,0,1:T(8,128)}) fusion(bf16[4,4,2,64,768]{4,3,1,2,0:T(8,128)(2,1)} %all-to-all-done, pred[]{:T(512)S(6)} %eq.31, pred[]{:T(512)S(6)} %eq.30, pred[]{:T(512)S(6)} %eq.29, pred[]{:T(512)S(6)} %eq.28, f32[4,1,64,768]{3,2,0,1:T(8,128)S(1)} %convolution_bitcast_fusion, ...), kind=kLoop, calls=%fused_computation.70 | loop fusion | flops 5505024 | bytes 7077892 | tf_op jit(solution)/shard_map/convert_element_type | solution.py:99
  83.9 3.7 %all-to-all-start.1 = ((bf16[4,2,64,768]{3,2,1,0:T(8,128)(2,1)}), bf16[4,2,64,768]{3,2,1,0:T(8,128)(2,1)S(1)}, u32[]{:S(2)}, u32[]{:S(2)}) async-start(bf16[4,2,64,768]{3,2,1,0:T(8,128)(2,1)} %copy.16), calls=%async_computation.1 | async-start | bytes 1572864 | tf_op jit(solution)/shard_map/all_to_all | solution.py:46
  87.7 8.3 %all-to-all-done.1 = bf16[4,2,64,768]{3,2,1,0:T(8,128)(2,1)S(1)} async-done(((bf16[4,2,64,768]{3,2,1,0:T(8,128)(2,1)}), bf16[4,2,64,768]{3,2,1,0:T(8,128)(2,1)S(1)}, u32[]{:S(2)}, u32[]{:S(2)}) %all-to-all-start.1) | async-done | bytes 786464 | tf_op jit(solution)/shard_map/all_to_all | solution.py:46
  98.6 3.7 %all-to-all-start.2 = ((bf16[16,64,768]{2,1,0:T(8,128)(2,1)}), bf16[16,64,768]{2,1,0:T(8,128)(2,1)S(1)}, u32[]{:S(2)}, u32[]{:S(2)}) async-start(bf16[16,64,768]{2,1,0:T(8,128)(2,1)} %broadcast_in_dim.25), calls=%async_computation.2 | async-start | bytes 3145728 | tf_op jit(solution)/shard_map/all_to_all | solution.py:106
  102.3 3.1 %collective-permute-start.3 = (bf16[64,768]{1,0:T(8,128)(2,1)S(1)}, bf16[64,768]{1,0:T(8,128)(2,1)S(1)}, u32[]{:S(2)}, u32[]{:S(2)}) collective-permute-start(bf16[64,768]{1,0:T(8,128)(2,1)S(1)} %fusion.31), channel_id=1, source_target_pairs={{0,128},{128,256},{256,384},{384,0},{32,160},{160,288},{288,416},{... | collective-permute-start | bytes 294920 | tf_op jit(solution)/shard_map/ppermute | solution.py:57
  105.5 4.3 %collective-permute-start.2 = (bf16[64,768]{1,0:T(8,128)(2,1)S(1)}, bf16[64,768]{1,0:T(8,128)(2,1)S(1)}, u32[]{:S(2)}, u32[]{:S(2)}) collective-permute-start(bf16[64,768]{1,0:T(8,128)(2,1)S(1)} %fusion.31), channel_id=1, source_target_pairs={{0,256},{128,384},{256,0},{384,128},{32,288},{160,416},{288,32},{4... | collective-permute-start | bytes 294920 | tf_op jit(solution)/shard_map/ppermute | solution.py:57
  109.8 3.1 %collective-permute-start.1 = (bf16[64,768]{1,0:T(8,128)(2,1)S(1)}, bf16[64,768]{1,0:T(8,128)(2,1)S(1)}, u32[]{:S(2)}, u32[]{:S(2)}) collective-permute-start(bf16[64,768]{1,0:T(8,128)(2,1)S(1)} %fusion.31), channel_id=1, source_target_pairs={{0,384},{128,0},{256,128},{384,256},{32,416},{160,32},{288,160},{4... | collective-permute-start | bytes 294920 | tf_op jit(solution)/shard_map/ppermute | solution.py:57
  112.9 11.3 %collective-permute-done.3 = bf16[64,768]{1,0:T(8,128)(2,1)S(1)} collective-permute-done((bf16[64,768]{1,0:T(8,128)(2,1)S(1)}, bf16[64,768]{1,0:T(8,128)(2,1)S(1)}, u32[]{:S(2)}, u32[]{:S(2)}) %collective-permute-start.3) | collective-permute-done | bytes 98336 | tf_op jit(solution)/shard_map/ppermute | solution.py:57
  126.1 5.0 %collective-permute-start.4 = (f32[16,32,384]{2,1,0:T(8,128)S(1)}, f32[16,32,384]{2,1,0:T(8,128)S(1)}, u32[]{:S(2)}, u32[]{:S(2)}) collective-permute-start(f32[16,32,384]{2,1,0:T(8,128)S(1)} %bitcast.139), channel_id=1, source_target_pairs={{0,1},{1,0},{2,3},{3,2},{4,5},{5,4},{6,7},{7,6},{8,9},{9,8},{10,11... | collective-permute-start | bytes 2359304 | tf_op jit(solution)/shard_map/ppermute | solution.py:109
  131.1 1.9 %collective-permute-done.4 = f32[16,32,384]{2,1,0:T(8,128)S(1)} collective-permute-done((f32[16,32,384]{2,1,0:T(8,128)S(1)}, f32[16,32,384]{2,1,0:T(8,128)S(1)}, u32[]{:S(2)}, u32[]{:S(2)}) %collective-permute-start.4) | collective-permute-done | bytes 786464 | tf_op jit(solution)/shard_map/ppermute | solution.py:109
  133.8 6.4 %all-to-all-start.3 = ((bf16[16,32,384]{2,1,0:T(8,128)(2,1)}), bf16[16,32,384]{2,1,0:T(8,128)(2,1)S(1)}, u32[]{:S(2)}, u32[]{:S(2)}) async-start(bf16[16,32,384]{2,1,0:T(8,128)(2,1)} %add_convert_fusion), calls=%async_computation.3 | async-start | bytes 786432 | tf_op jit(solution)/shard_map/all_to_all | solution.py:111
  140.2 1.8 %fusion.41 = f32[384,768]{1,0:T(8,128)} fusion(bf16[1024,384]{1,0:T(8,128)(2,1)S(1)} %bitcast.125, bf16[1024,768]{1,0:T(8,128)(2,1)S(1)} %bitcast.122), kind=kOutput, calls=%fused_computation.73 | convolution fusion | flops 603979776 | bytes 3538944 | tf_op jit(solution)/shard_map/dot_general | solution.py:24
  142.0 1.9 %collective-permute-start.7 = (bf16[256,768]{1,0:T(8,128)(2,1)}, bf16[256,768]{1,0:T(8,128)(2,1)S(1)}, u32[]{:S(2)}, u32[]{:S(2)}) collective-permute-start(bf16[256,768]{1,0:T(8,128)(2,1)} %pad_maximum_fusion.3), channel_id=1, source_target_pairs={{0,32},{32,64},{64,96},{96,0},{128,160},{160,192},{192,224},{224,1... | collective-permute-start | bytes 1179656 | tf_op jit(solution)/shard_map/ppermute | solution.py:57
  144.0 3.6 %collective-permute-start.6 = (bf16[256,768]{1,0:T(8,128)(2,1)}, bf16[256,768]{1,0:T(8,128)(2,1)S(1)}, u32[]{:S(2)}, u32[]{:S(2)}) collective-permute-start(bf16[256,768]{1,0:T(8,128)(2,1)} %pad_maximum_fusion.3), channel_id=1, source_target_pairs={{0,64},{32,96},{64,0},{96,32},{128,192},{160,224},{192,128},{224,1... | collective-permute-start | bytes 1179656 | tf_op jit(solution)/shard_map/ppermute | solution.py:57
  147.6 2.9 %collective-permute-start.5 = (bf16[256,768]{1,0:T(8,128)(2,1)}, bf16[256,768]{1,0:T(8,128)(2,1)S(1)}, u32[]{:S(2)}, u32[]{:S(2)}) collective-permute-start(bf16[256,768]{1,0:T(8,128)(2,1)} %pad_maximum_fusion.3), channel_id=1, source_target_pairs={{0,96},{32,0},{64,32},{96,64},{128,224},{160,128},{192,160},{224,1... | collective-permute-start | bytes 1179656 | tf_op jit(solution)/shard_map/ppermute | solution.py:57
  152.3 4.2 %collective-permute-done.7 = bf16[256,768]{1,0:T(8,128)(2,1)S(1)} collective-permute-done((bf16[256,768]{1,0:T(8,128)(2,1)}, bf16[256,768]{1,0:T(8,128)(2,1)S(1)}, u32[]{:S(2)}, u32[]{:S(2)}) %collective-permute-start.7) | collective-permute-done | bytes 393248 | tf_op jit(solution)/shard_map/ppermute | solution.py:57
  156.5 2.5 %collective-permute-done.5 = bf16[256,768]{1,0:T(8,128)(2,1)S(1)} collective-permute-done((bf16[256,768]{1,0:T(8,128)(2,1)}, bf16[256,768]{1,0:T(8,128)(2,1)S(1)}, u32[]{:S(2)}, u32[]{:S(2)}) %collective-permute-start.5) | collective-permute-done | bytes 393248 | tf_op jit(solution)/shard_map/ppermute | solution.py:57
  159.0 3.0 %fusion.3 = f32[768,384]{1,0:T(8,128)} fusion(bf16[1024,384]{1,0:T(8,128)(2,1)S(1)} %bitcast.138, bf16[256,768]{1,0:T(8,128)(2,1)S(1)} %collective-permute-done.7, bf16[256,768]{1,0:T(8,128)(2,1)S(1)} %collective-permute-done.6, bf16[256,768]{1,0:T(8,128)(2,1)S(1)} %collective-permute-done.5, bf16[256,768]{1,0:T(8,128)(2,1)} %pad_maximum_fusion.3), kind=kOutput, calls=%fused_computation.7 | convolution fusion | flops 610271232 | bytes 3538944 | tf_op jit(solution)/shard_map/dot_general | solution.py:24
  (37 shorter events, 15.8 us)
Async XLA Ops:
  0.6 49.8 %copy-start = (bf16[384,768]{1,0:T(8,128)(2,1)S(1)}, bf16[384,768]{1,0:T(8,128)(2,1)}, u32[]{:S(2)}) copy-start(bf16[384,768]{1,0:T(8,128)(2,1)} %param.6) | copy-start | bytes 1769476
  35.5 11.5 %collective-permute-start = (bf16[16,2,32,384]{3,2,0,1:T(8,128)(2,1)S(1)}, bf16[16,2,32,384]{3,2,0,1:T(8,128)(2,1)S(1)}, u32[]{:S(2)}, u32[]{:S(2)}) collective-permute-start(bf16[16,2,32,384]{3,2,0,1:T(8,128)(2,1)S(1)} %copy.12), channel_id=1, source_target_pairs={{0,1},{1,0},{2,3},{3,2},{4,5},{5,4},{6,7},{7,6},{8,9},{9,8},{10,11... | collective-permute-start | bytes 2359304 | tf_op jit(solution)/shard_map/ppermute | solution.py:75
  47.3 1.2 copy-start.3
  47.4 10.7 %copy-start.1 = (bf16[4,4,64,384]{3,2,1,0:T(8,128)(2,1)}, bf16[4,4,64,384]{3,2,1,0:T(8,128)(2,1)S(1)}, u32[]{:S(2)}) copy-start(bf16[4,4,64,384]{3,2,1,0:T(8,128)(2,1)S(1)} %copy_select_fusion) | copy-start | bytes 2359300
  49.6 0.9 copy-start.2
  53.4 26.0 %all-to-all-start = ((bf16[4,4,2,64,768]{4,3,1,2,0:T(8,128)(2,1)}), bf16[4,4,2,64,768]{4,3,1,2,0:T(8,128)(2,1)}, u32[]{:S(2)}, u32[]{:S(2)}) async-start(bf16[4,4,2,64,768]{4,3,1,2,0:T(8,128)(2,1)} %pad_maximum_fusion), calls=%async_computation | async-start | bytes 6291456 | tf_op jit(solution)/shard_map/all_to_all | solution.py:46
  83.9 12.1 %all-to-all-start.1 = ((bf16[4,2,64,768]{3,2,1,0:T(8,128)(2,1)}), bf16[4,2,64,768]{3,2,1,0:T(8,128)(2,1)S(1)}, u32[]{:S(2)}, u32[]{:S(2)}) async-start(bf16[4,2,64,768]{3,2,1,0:T(8,128)(2,1)} %copy.16), calls=%async_computation.1 | async-start | bytes 1572864 | tf_op jit(solution)/shard_map/all_to_all | solution.py:46
  98.6 26.4 %all-to-all-start.2 = ((bf16[16,64,768]{2,1,0:T(8,128)(2,1)}), bf16[16,64,768]{2,1,0:T(8,128)(2,1)S(1)}, u32[]{:S(2)}, u32[]{:S(2)}) async-start(bf16[16,64,768]{2,1,0:T(8,128)(2,1)} %broadcast_in_dim.25), calls=%async_computation.2 | async-start | bytes 3145728 | tf_op jit(solution)/shard_map/all_to_all | solution.py:106
  102.3 21.8 %collective-permute-start.3 = (bf16[64,768]{1,0:T(8,128)(2,1)S(1)}, bf16[64,768]{1,0:T(8,128)(2,1)S(1)}, u32[]{:S(2)}, u32[]{:S(2)}) collective-permute-start(bf16[64,768]{1,0:T(8,128)(2,1)S(1)} %fusion.31), channel_id=1, source_target_pairs={{0,128},{128,256},{256,384},{384,0},{32,160},{160,288},{288,416},{... | collective-permute-start | bytes 294920 | tf_op jit(solution)/shard_map/ppermute | solution.py:57
  105.5 18.7 %collective-permute-start.2 = (bf16[64,768]{1,0:T(8,128)(2,1)S(1)}, bf16[64,768]{1,0:T(8,128)(2,1)S(1)}, u32[]{:S(2)}, u32[]{:S(2)}) collective-permute-start(bf16[64,768]{1,0:T(8,128)(2,1)S(1)} %fusion.31), channel_id=1, source_target_pairs={{0,256},{128,384},{256,0},{384,128},{32,288},{160,416},{288,32},{4... | collective-permute-start | bytes 294920 | tf_op jit(solution)/shard_map/ppermute | solution.py:57
  109.8 14.4 %collective-permute-start.1 = (bf16[64,768]{1,0:T(8,128)(2,1)S(1)}, bf16[64,768]{1,0:T(8,128)(2,1)S(1)}, u32[]{:S(2)}, u32[]{:S(2)}) collective-permute-start(bf16[64,768]{1,0:T(8,128)(2,1)S(1)} %fusion.31), channel_id=1, source_target_pairs={{0,384},{128,0},{256,128},{384,256},{32,416},{160,32},{288,160},{4... | collective-permute-start | bytes 294920 | tf_op jit(solution)/shard_map/ppermute | solution.py:57
  126.1 6.9 %collective-permute-start.4 = (f32[16,32,384]{2,1,0:T(8,128)S(1)}, f32[16,32,384]{2,1,0:T(8,128)S(1)}, u32[]{:S(2)}, u32[]{:S(2)}) collective-permute-start(f32[16,32,384]{2,1,0:T(8,128)S(1)} %bitcast.139), channel_id=1, source_target_pairs={{0,1},{1,0},{2,3},{3,2},{4,5},{5,4},{6,7},{7,6},{8,9},{9,8},{10,11... | collective-permute-start | bytes 2359304 | tf_op jit(solution)/shard_map/ppermute | solution.py:109
  133.8 28.2 %all-to-all-start.3 = ((bf16[16,32,384]{2,1,0:T(8,128)(2,1)}), bf16[16,32,384]{2,1,0:T(8,128)(2,1)S(1)}, u32[]{:S(2)}, u32[]{:S(2)}) async-start(bf16[16,32,384]{2,1,0:T(8,128)(2,1)} %add_convert_fusion), calls=%async_computation.3 | async-start | bytes 786432 | tf_op jit(solution)/shard_map/all_to_all | solution.py:111
  142.0 14.4 %collective-permute-start.7 = (bf16[256,768]{1,0:T(8,128)(2,1)}, bf16[256,768]{1,0:T(8,128)(2,1)S(1)}, u32[]{:S(2)}, u32[]{:S(2)}) collective-permute-start(bf16[256,768]{1,0:T(8,128)(2,1)} %pad_maximum_fusion.3), channel_id=1, source_target_pairs={{0,32},{32,64},{64,96},{96,0},{128,160},{160,192},{192,224},{224,1... | collective-permute-start | bytes 1179656 | tf_op jit(solution)/shard_map/ppermute | solution.py:57
  144.0 12.5 %collective-permute-start.6 = (bf16[256,768]{1,0:T(8,128)(2,1)}, bf16[256,768]{1,0:T(8,128)(2,1)S(1)}, u32[]{:S(2)}, u32[]{:S(2)}) collective-permute-start(bf16[256,768]{1,0:T(8,128)(2,1)} %pad_maximum_fusion.3), channel_id=1, source_target_pairs={{0,64},{32,96},{64,0},{96,32},{128,192},{160,224},{192,128},{224,1... | collective-permute-start | bytes 1179656 | tf_op jit(solution)/shard_map/ppermute | solution.py:57
  147.6 11.4 %collective-permute-start.5 = (bf16[256,768]{1,0:T(8,128)(2,1)}, bf16[256,768]{1,0:T(8,128)(2,1)S(1)}, u32[]{:S(2)}, u32[]{:S(2)}) collective-permute-start(bf16[256,768]{1,0:T(8,128)(2,1)} %pad_maximum_fusion.3), channel_id=1, source_target_pairs={{0,96},{32,0},{64,32},{96,64},{128,224},{160,128},{192,160},{224,1... | collective-permute-start | bytes 1179656 | tf_op jit(solution)/shard_map/ppermute | solution.py:57

commit v8 on v7

--- a/solution.py
+++ b/solution.py
@@ -42,12 +42,8 @@
     return groups
 
 
-def add_ring(blocks, own, pos, axis):
-    landed = lax.all_to_all(blocks, PLANE, 0, 0, tiled=True, axis_index_groups=rings(axis))
-    total = own
-    for i in range(4):
-        total = total + jnp.where(i == pos, 0.0, landed[i].astype(jnp.float32))
-    return total
+def swap_ring(blocks, axis):
+    return lax.all_to_all(blocks, PLANE, 0, 0, tiled=True, axis_index_groups=rings(axis))
 
 
 def hop(value, axis, step):
@@ -90,13 +86,11 @@
     pre_part = dot(x_ring.reshape(flat), weight_in, 1, 0).astype(jnp.bfloat16)
     grad_part = dot(g_ring.reshape(flat), weight_out, 1, 1).astype(jnp.bfloat16)
     parts = [part.reshape(4, 4, share, hidden) for part in (pre_part, grad_part)]
-    own_x = lax.dynamic_index_in_dim(x_ring, pos_a, 0, keepdims=False).reshape(flat)
-    own_g = lax.dynamic_index_in_dim(g_ring, pos_a, 0, keepdims=False).reshape(flat)
-    own_parts = [dot(own_x, weight_in, 1, 0), dot(own_g, weight_out, 1, 1)]
-    own_parts = [part.reshape(4, share, hidden) for part in own_parts]
-    line = add_ring(jnp.stack(parts, axis=2), jnp.stack(own_parts, axis=1), pos_a, 0)
-    own_line = lax.dynamic_index_in_dim(line, pos_b, 0, keepdims=False)
-    sums = add_ring(line.astype(jnp.bfloat16), own_line, pos_b, 1)
+    line = add_blocks(swap_ring(jnp.stack(parts, axis=2), 0))
+    sums = lax.dynamic_index_in_dim(line, pos_b, 0, keepdims=False)
+    landed = swap_ring(line.astype(jnp.bfloat16), 1)
+    for i in range(4):
+        sums = sums + jnp.where(i == pos_b, 0.0, landed[i].astype(jnp.float32))
     preact, act_grad = sums[0], sums[1]
 
     activated = (preact * normal_cdf(preact)).astype(jnp.bfloat16)

time: 164 us -> 159 us (0.970)
  blocking collectives: 33.9 us -> 59.1 us
  waiting for transfers between devices: 49.6 us -> 30.1 us
  starting transfers between devices: 52 us -> 47.3 us
  other arithmetic: 12.2 us -> 8.49 us
  matrix products: 9.49 us -> 7.82 us
    all_to_all x0 -> x1, blocking collectives: none -> 25.3 us  [swap_ring(): lax.all_to_all(blocks, PLANE, 0, 0, tiled=True, axis_index_groups=rings(a...]
    all_to_all x2 -> x1, waiting for transfers between devices: 27.9 us -> 8.34 us  [swap_ring(): lax.all_to_all(blocks, PLANE, 0, 0, tiled=True, axis_index_groups=rings(a...]
    all_to_all x2 -> x1, starting transfers between devices: 8.37 us -> 3.72 us  [swap_ring(): lax.all_to_all(blocks, PLANE, 0, 0, tiled=True, axis_index_groups=rings(a...]
    convert_element_type x1 -> x0, other arithmetic: 3.65 us -> none  [body(): sums = add_ring(line.astype(jnp.bfloat16), own_line, pos_b, 1)]
    dot_general x7 -> x5, matrix products: 9.49 us -> 7.82 us  [dot(): lax.dot_general(a, b, (((ca,), (cb,)), ((), ())), preferred_element_type=...]
    another operation x1, other arithmetic: 1.95 us -> 0.29 us  [body(): line = add_blocks(swap_ring(jnp.stack(parts, axis=2), 0))]
  transfers between devices with their start and end apart: 12 -> 11, of which waited for: 7 -> 6; matrix products, arithmetic and copies ran while one was open for 6% -> 5% of each run, Pallas kernels for 0% -> 0%
where the time goes in v8:
time: 159 us; the launch traced here: 157 us
  blocking collectives  59.1 us (37%)
  starting transfers between devices  47.3 us (30%)
  waiting for transfers between devices  30.1 us (19%)
  other arithmetic  8.49 us (5%)
  matrix products  7.82 us (5%)
  local copies, waits for them, and re-layouts  3.76 us (2%)
    all_gather x1, blocking collectives, body(): own = lax.all_gather(jnp.stack([inputs, cotangent]), 'z', axis=0)  33.9 us
    all_to_all x1, blocking collectives, swap_ring(): lax.all_to_all(blocks, PLANE, 0, 0, tiled=True, axis_index_groups=rings(a...  25.3 us
    ppermute x6, starting transfers between devices, hop(): return lax.ppermute(value, PLANE, pairs)  18.9 us
    ppermute x6, waiting for transfers between devices, hop(): return lax.ppermute(value, PLANE, pairs)  18 us
    ppermute x1, starting transfers between devices, body(): other = lax.ppermute(own, 'core', SWAP)  9.64 us
    all_to_all x1, waiting for transfers between devices, swap_ring(): lax.all_to_all(blocks, PLANE, 0, 0, tiled=True, axis_index_groups=rings(a...  8.34 us
    dot_general x5, matrix products, dot(): lax.dot_general(a, b, (((ca,), (cb,)), ((), ())), preferred_element_type=...  7.82 us
    all_to_all x1, starting transfers between devices, body(): pieces = lax.all_to_all(chip, 'z', 0, 0, tiled=True)  6.37 us
  transfers between devices with their start and end apart: 11, of which 6 were waited for; matrix products, arithmetic and copies ran while one was open for 5% of the time, Pallas kernels for 0%

profile of v8, /device:TPU:1, one launch (start us, length us, event | category | flops | bytes accessed | tf_op | source)
XLA Modules:
  0.0 157.5 jit_solution(15670013445646455013)
XLA Ops:
  1.5 33.9 %all-gather = bf16[32,32,384]{2,1,0:T(8,128)(2,1)S(1)} all-gather(bf16[2,32,384]{2,1,0:T(8,128)(2,1)S(1)} %pad_maximum_fusion.4), channel_id=2, replica_groups=mesh['y'=4,'x'=4,'z'=16,'core'=2] {'z'}, dimensions={0}, use_global_device_ids=true | all-gather | bytes 835584 | tf_op jit(solution)/shard_map/all_gather | solution.py:70
  35.5 9.6 %collective-permute-start = (bf16[16,2,32,384]{3,2,0,1:T(8,128)(2,1)S(1)}, bf16[16,2,32,384]{3,2,0,1:T(8,128)(2,1)S(1)}, u32[]{:S(2)}, u32[]{:S(2)}) collective-permute-start(bf16[16,2,32,384]{3,2,0,1:T(8,128)(2,1)S(1)} %copy.12), channel_id=1, source_target_pairs={{0,1},{1,0},{2,3},{3,2},{4,5},{5,4},{6,7},{7,6},{8,9},{9,8},{10,11... | collective-permute-start | bytes 2359304 | tf_op jit(solution)/shard_map/ppermute | solution.py:71
  45.2 1.8 %collective-permute-done = bf16[16,2,32,384]{3,2,0,1:T(8,128)(2,1)S(1)} collective-permute-done((bf16[16,2,32,384]{3,2,0,1:T(8,128)(2,1)S(1)}, bf16[16,2,32,384]{3,2,0,1:T(8,128)(2,1)S(1)}, u32[]{:S(2)}, u32[]{:S(2)}) %collective-permute-start) | collective-permute-done | bytes 786464 | tf_op jit(solution)/shard_map/ppermute | solution.py:71
  50.9 25.3 %all_to_all.20 = bf16[4,4,2,64,768]{4,3,1,2,0:T(8,128)(2,1)S(1)} all-to-all(bf16[4,4,2,64,768]{4,3,1,2,0:T(8,128)(2,1)S(1)} %pad_maximum_fusion), channel_id=1, replica_groups={{0,32,64,96},{128,160,192,224},{256,288,320,352},{384,416,448,480},{1,1..., dimensions={0} | all-to-all | bytes 6291456 | tf_op jit(solution)/shard_map/all_to_all | solution.py:46
  76.2 1.6 %convert_bitcast_fusion = (bf16[4,2,64,768]{3,2,0,1:T(8,128)(2,1)S(1)}, f32[1,4,2,64,768]{4,3,1,2,0:T(8,128)}) fusion(bf16[4,4,2,64,768]{4,3,1,2,0:T(8,128)(2,1)S(1)} %all_to_all.20), kind=kLoop, calls=%fused_computation.23 | loop fusion | flops 3145728 | bytes 5505024 | tf_op jit(solution)/shard_map/add | solution.py:30
  78.7 3.7 %all-to-all-start.1 = ((bf16[4,2,64,768]{3,2,1,0:T(8,128)(2,1)}), bf16[4,2,64,768]{3,2,1,0:T(8,128)(2,1)S(1)}, u32[]{:S(2)}, u32[]{:S(2)}) async-start(bf16[4,2,64,768]{3,2,1,0:T(8,128)(2,1)} %copy.18), calls=%async_computation.1 | async-start | bytes 1572864 | tf_op jit(solution)/shard_map/all_to_all | solution.py:46
  82.4 8.3 %all-to-all-done.1 = bf16[4,2,64,768]{3,2,1,0:T(8,128)(2,1)S(1)} async-done(((bf16[4,2,64,768]{3,2,1,0:T(8,128)(2,1)}), bf16[4,2,64,768]{3,2,1,0:T(8,128)(2,1)S(1)}, u32[]{:S(2)}, u32[]{:S(2)}) %all-to-all-start.1) | async-done | bytes 786464 | tf_op jit(solution)/shard_map/all_to_all | solution.py:46
  92.0 1.3 broadcast_in_dim.17
  93.4 3.7 %all-to-all-start.2 = ((bf16[16,64,768]{2,1,0:T(8,128)(2,1)}), bf16[16,64,768]{2,1,0:T(8,128)(2,1)S(1)}, u32[]{:S(2)}, u32[]{:S(2)}) async-start(bf16[16,64,768]{2,1,0:T(8,128)(2,1)} %broadcast_in_dim.17), calls=%async_computation.2 | async-start | bytes 3145728 | tf_op jit(solution)/shard_map/all_to_all | solution.py:100
  97.1 3.1 %collective-permute-start.3 = (bf16[64,768]{1,0:T(8,128)(2,1)S(1)}, bf16[64,768]{1,0:T(8,128)(2,1)S(1)}, u32[]{:S(2)}, u32[]{:S(2)}) collective-permute-start(bf16[64,768]{1,0:T(8,128)(2,1)S(1)} %fusion.25), channel_id=1, source_target_pairs={{0,128},{128,256},{256,384},{384,0},{32,160},{160,288},{288,416},{... | collective-permute-start | bytes 294920 | tf_op jit(solution)/shard_map/ppermute | solution.py:53
  100.3 4.3 %collective-permute-start.2 = (bf16[64,768]{1,0:T(8,128)(2,1)S(1)}, bf16[64,768]{1,0:T(8,128)(2,1)S(1)}, u32[]{:S(2)}, u32[]{:S(2)}) collective-permute-start(bf16[64,768]{1,0:T(8,128)(2,1)S(1)} %fusion.25), channel_id=1, source_target_pairs={{0,256},{128,384},{256,0},{384,128},{32,288},{160,416},{288,32},{4... | collective-permute-start | bytes 294920 | tf_op jit(solution)/shard_map/ppermute | solution.py:53
  104.6 3.1 %collective-permute-start.1 = (bf16[64,768]{1,0:T(8,128)(2,1)S(1)}, bf16[64,768]{1,0:T(8,128)(2,1)S(1)}, u32[]{:S(2)}, u32[]{:S(2)}) collective-permute-start(bf16[64,768]{1,0:T(8,128)(2,1)S(1)} %fusion.25), channel_id=1, source_target_pairs={{0,384},{128,0},{256,128},{384,256},{32,416},{160,32},{288,160},{4... | collective-permute-start | bytes 294920 | tf_op jit(solution)/shard_map/ppermute | solution.py:53
  107.7 11.3 %collective-permute-done.3 = bf16[64,768]{1,0:T(8,128)(2,1)S(1)} collective-permute-done((bf16[64,768]{1,0:T(8,128)(2,1)S(1)}, bf16[64,768]{1,0:T(8,128)(2,1)S(1)}, u32[]{:S(2)}, u32[]{:S(2)}) %collective-permute-start.3) | collective-permute-done | bytes 98336 | tf_op jit(solution)/shard_map/ppermute | solution.py:53
  120.9 5.0 %collective-permute-start.4 = (f32[16,32,384]{2,1,0:T(8,128)S(1)}, f32[16,32,384]{2,1,0:T(8,128)S(1)}, u32[]{:S(2)}, u32[]{:S(2)}) collective-permute-start(f32[16,32,384]{2,1,0:T(8,128)S(1)} %bitcast.105), channel_id=1, source_target_pairs={{0,1},{1,0},{2,3},{3,2},{4,5},{5,4},{6,7},{7,6},{8,9},{9,8},{10,11... | collective-permute-start | bytes 2359304 | tf_op jit(solution)/shard_map/ppermute | solution.py:103
  125.9 1.9 %collective-permute-done.4 = f32[16,32,384]{2,1,0:T(8,128)S(1)} collective-permute-done((f32[16,32,384]{2,1,0:T(8,128)S(1)}, f32[16,32,384]{2,1,0:T(8,128)S(1)}, u32[]{:S(2)}, u32[]{:S(2)}) %collective-permute-start.4) | collective-permute-done | bytes 786464 | tf_op jit(solution)/shard_map/ppermute | solution.py:103
  128.6 6.4 %all-to-all-start.3 = ((bf16[16,32,384]{2,1,0:T(8,128)(2,1)}), bf16[16,32,384]{2,1,0:T(8,128)(2,1)S(1)}, u32[]{:S(2)}, u32[]{:S(2)}) async-start(bf16[16,32,384]{2,1,0:T(8,128)(2,1)} %add_convert_fusion), calls=%async_computation.3 | async-start | bytes 786432 | tf_op jit(solution)/shard_map/all_to_all | solution.py:105
  135.0 1.8 %fusion.31 = f32[384,768]{1,0:T(8,128)} fusion(bf16[1024,384]{1,0:T(8,128)(2,1)S(1)} %bitcast.94, bf16[1024,768]{1,0:T(8,128)(2,1)S(1)} %bitcast.91), kind=kOutput, calls=%fused_computation.59 | convolution fusion | flops 603979776 | bytes 3538944 | tf_op jit(solution)/shard_map/dot_general | solution.py:24
  136.8 1.9 %collective-permute-start.7 = (bf16[256,768]{1,0:T(8,128)(2,1)}, bf16[256,768]{1,0:T(8,128)(2,1)S(1)}, u32[]{:S(2)}, u32[]{:S(2)}) collective-permute-start(bf16[256,768]{1,0:T(8,128)(2,1)} %pad_maximum_fusion.3), channel_id=1, source_target_pairs={{0,32},{32,64},{64,96},{96,0},{128,160},{160,192},{192,224},{224,1... | collective-permute-start | bytes 1179656 | tf_op jit(solution)/shard_map/ppermute | solution.py:53
  138.7 3.7 %collective-permute-start.6 = (bf16[256,768]{1,0:T(8,128)(2,1)}, bf16[256,768]{1,0:T(8,128)(2,1)S(1)}, u32[]{:S(2)}, u32[]{:S(2)}) collective-permute-start(bf16[256,768]{1,0:T(8,128)(2,1)} %pad_maximum_fusion.3), channel_id=1, source_target_pairs={{0,64},{32,96},{64,0},{96,32},{128,192},{160,224},{192,128},{224,1... | collective-permute-start | bytes 1179656 | tf_op jit(solution)/shard_map/ppermute | solution.py:53
  142.4 2.8 %collective-permute-start.5 = (bf16[256,768]{1,0:T(8,128)(2,1)}, bf16[256,768]{1,0:T(8,128)(2,1)S(1)}, u32[]{:S(2)}, u32[]{:S(2)}) collective-permute-start(bf16[256,768]{1,0:T(8,128)(2,1)} %pad_maximum_fusion.3), channel_id=1, source_target_pairs={{0,96},{32,0},{64,32},{96,64},{128,224},{160,128},{192,160},{224,1... | collective-permute-start | bytes 1179656 | tf_op jit(solution)/shard_map/ppermute | solution.py:53
  145.3 1.5 fusion.9
  147.1 4.2 %collective-permute-done.7 = bf16[256,768]{1,0:T(8,128)(2,1)S(1)} collective-permute-done((bf16[256,768]{1,0:T(8,128)(2,1)}, bf16[256,768]{1,0:T(8,128)(2,1)S(1)}, u32[]{:S(2)}, u32[]{:S(2)}) %collective-permute-start.7) | collective-permute-done | bytes 393248 | tf_op jit(solution)/shard_map/ppermute | solution.py:53
  151.3 2.5 %collective-permute-done.5 = bf16[256,768]{1,0:T(8,128)(2,1)S(1)} collective-permute-done((bf16[256,768]{1,0:T(8,128)(2,1)}, bf16[256,768]{1,0:T(8,128)(2,1)S(1)}, u32[]{:S(2)}, u32[]{:S(2)}) %collective-permute-start.5) | collective-permute-done | bytes 393248 | tf_op jit(solution)/shard_map/ppermute | solution.py:53
  153.8 3.0 %fusion = f32[768,384]{1,0:T(8,128)} fusion(bf16[1024,384]{1,0:T(8,128)(2,1)S(1)} %bitcast.104, bf16[256,768]{1,0:T(8,128)(2,1)S(1)} %collective-permute-done.7, bf16[256,768]{1,0:T(8,128)(2,1)S(1)} %collective-permute-done.6, bf16[256,768]{1,0:T(8,128)(2,1)S(1)} %collective-permute-done.5, bf16[256,768]{1,0:T(8,128)(2,1)} %pad_maximum_fusion.3), kind=kOutput, calls=%fused_computation.3 | convolution fusion | flops 610271232 | bytes 3538944 | tf_op jit(solution)/shard_map/dot_general | solution.py:24
  (32 shorter events, 10.8 us)
Async XLA Ops:
  0.6 49.0 %copy-start = (bf16[384,768]{1,0:T(8,128)(2,1)S(1)}, bf16[384,768]{1,0:T(8,128)(2,1)}, u32[]{:S(2)}) copy-start(bf16[384,768]{1,0:T(8,128)(2,1)} %param.6) | copy-start | bytes 1769476
  35.5 11.5 %collective-permute-start = (bf16[16,2,32,384]{3,2,0,1:T(8,128)(2,1)S(1)}, bf16[16,2,32,384]{3,2,0,1:T(8,128)(2,1)S(1)}, u32[]{:S(2)}, u32[]{:S(2)}) collective-permute-start(bf16[16,2,32,384]{3,2,0,1:T(8,128)(2,1)S(1)} %copy.12), channel_id=1, source_target_pairs={{0,1},{1,0},{2,3},{3,2},{4,5},{5,4},{6,7},{7,6},{8,9},{9,8},{10,11... | collective-permute-start | bytes 2359304 | tf_op jit(solution)/shard_map/ppermute | solution.py:71
  47.3 1.2 copy-start.2
  47.4 2.3 %copy-start.1 = (bf16[4,4,64,384]{3,2,1,0:T(8,128)(2,1)}, bf16[4,4,64,384]{3,2,1,0:T(8,128)(2,1)S(1)}, u32[]{:S(2)}) copy-start(bf16[4,4,64,384]{3,2,1,0:T(8,128)(2,1)S(1)} %bitcast_select_fusion) | copy-start | bytes 2359300
  78.7 12.1 %all-to-all-start.1 = ((bf16[4,2,64,768]{3,2,1,0:T(8,128)(2,1)}), bf16[4,2,64,768]{3,2,1,0:T(8,128)(2,1)S(1)}, u32[]{:S(2)}, u32[]{:S(2)}) async-start(bf16[4,2,64,768]{3,2,1,0:T(8,128)(2,1)} %copy.18), calls=%async_computation.1 | async-start | bytes 1572864 | tf_op jit(solution)/shard_map/all_to_all | solution.py:46
  93.4 26.5 %all-to-all-start.2 = ((bf16[16,64,768]{2,1,0:T(8,128)(2,1)}), bf16[16,64,768]{2,1,0:T(8,128)(2,1)S(1)}, u32[]{:S(2)}, u32[]{:S(2)}) async-start(bf16[16,64,768]{2,1,0:T(8,128)(2,1)} %broadcast_in_dim.17), calls=%async_computation.2 | async-start | bytes 3145728 | tf_op jit(solution)/shard_map/all_to_all | solution.py:100
  97.1 21.9 %collective-permute-start.3 = (bf16[64,768]{1,0:T(8,128)(2,1)S(1)}, bf16[64,768]{1,0:T(8,128)(2,1)S(1)}, u32[]{:S(2)}, u32[]{:S(2)}) collective-permute-start(bf16[64,768]{1,0:T(8,128)(2,1)S(1)} %fusion.25), channel_id=1, source_target_pairs={{0,128},{128,256},{256,384},{384,0},{32,160},{160,288},{288,416},{... | collective-permute-start | bytes 294920 | tf_op jit(solution)/shard_map/ppermute | solution.py:53
  100.3 18.7 %collective-permute-start.2 = (bf16[64,768]{1,0:T(8,128)(2,1)S(1)}, bf16[64,768]{1,0:T(8,128)(2,1)S(1)}, u32[]{:S(2)}, u32[]{:S(2)}) collective-permute-start(bf16[64,768]{1,0:T(8,128)(2,1)S(1)} %fusion.25), channel_id=1, source_target_pairs={{0,256},{128,384},{256,0},{384,128},{32,288},{160,416},{288,32},{4... | collective-permute-start | bytes 294920 | tf_op jit(solution)/shard_map/ppermute | solution.py:53
  104.6 14.4 %collective-permute-start.1 = (bf16[64,768]{1,0:T(8,128)(2,1)S(1)}, bf16[64,768]{1,0:T(8,128)(2,1)S(1)}, u32[]{:S(2)}, u32[]{:S(2)}) collective-permute-start(bf16[64,768]{1,0:T(8,128)(2,1)S(1)} %fusion.25), channel_id=1, source_target_pairs={{0,384},{128,0},{256,128},{384,256},{32,416},{160,32},{288,160},{4... | collective-permute-start | bytes 294920 | tf_op jit(solution)/shard_map/ppermute | solution.py:53
  120.9 6.9 %collective-permute-start.4 = (f32[16,32,384]{2,1,0:T(8,128)S(1)}, f32[16,32,384]{2,1,0:T(8,128)S(1)}, u32[]{:S(2)}, u32[]{:S(2)}) collective-permute-start(f32[16,32,384]{2,1,0:T(8,128)S(1)} %bitcast.105), channel_id=1, source_target_pairs={{0,1},{1,0},{2,3},{3,2},{4,5},{5,4},{6,7},{7,6},{8,9},{9,8},{10,11... | collective-permute-start | bytes 2359304 | tf_op jit(solution)/shard_map/ppermute | solution.py:103
  128.6 28.2 %all-to-all-start.3 = ((bf16[16,32,384]{2,1,0:T(8,128)(2,1)}), bf16[16,32,384]{2,1,0:T(8,128)(2,1)S(1)}, u32[]{:S(2)}, u32[]{:S(2)}) async-start(bf16[16,32,384]{2,1,0:T(8,128)(2,1)} %add_convert_fusion), calls=%async_computation.3 | async-start | bytes 786432 | tf_op jit(solution)/shard_map/all_to_all | solution.py:105
  136.8 14.4 %collective-permute-start.7 = (bf16[256,768]{1,0:T(8,128)(2,1)}, bf16[256,768]{1,0:T(8,128)(2,1)S(1)}, u32[]{:S(2)}, u32[]{:S(2)}) collective-permute-start(bf16[256,768]{1,0:T(8,128)(2,1)} %pad_maximum_fusion.3), channel_id=1, source_target_pairs={{0,32},{32,64},{64,96},{96,0},{128,160},{160,192},{192,224},{224,1... | collective-permute-start | bytes 1179656 | tf_op jit(solution)/shard_map/ppermute | solution.py:53
  138.7 12.5 %collective-permute-start.6 = (bf16[256,768]{1,0:T(8,128)(2,1)}, bf16[256,768]{1,0:T(8,128)(2,1)S(1)}, u32[]{:S(2)}, u32[]{:S(2)}) collective-permute-start(bf16[256,768]{1,0:T(8,128)(2,1)} %pad_maximum_fusion.3), channel_id=1, source_target_pairs={{0,64},{32,96},{64,0},{96,32},{128,192},{160,224},{192,128},{224,1... | collective-permute-start | bytes 1179656 | tf_op jit(solution)/shard_map/ppermute | solution.py:53
  142.4 11.4 %collective-permute-start.5 = (bf16[256,768]{1,0:T(8,128)(2,1)}, bf16[256,768]{1,0:T(8,128)(2,1)S(1)}, u32[]{:S(2)}, u32[]{:S(2)}) collective-permute-start(bf16[256,768]{1,0:T(8,128)(2,1)} %pad_maximum_fusion.3), channel_id=1, source_target_pairs={{0,96},{32,0},{64,32},{96,64},{128,224},{160,128},{192,160},{224,1... | collective-permute-start | bytes 1179656 | tf_op jit(solution)/shard_map/ppermute | solution.py:53
